TPU v7x, 256 devices: a whole 4x4x8 slice. The times are simulated.
256 devices in a mesh: seq: 32 (over y, z_lo, core), head: 8 (over x, z_hi).
Axes of the slice: x: 4, y: 4, z: 8 (z_hi: 2, z_lo: 4; z = z_hi * 4 + z_lo), core: 2. Of those that a mesh axis runs over, the one named last changes fastest.
Arguments:
- stream: bfloat16 [6144, 5120], P('seq', 'head'), may hold values from -57 to 57
- normed: bfloat16 [6144, 5120], P('seq', 'head'), may hold values from -41 to 41
- qkv_weight: bfloat16 [5120, 3, 3072], P(None, None, 'head'), may hold values from -0.078125 to 0.078125
- out_weight: bfloat16 [3072, 5120], P('head', 'seq'), may hold values from -0.109375 to 0.109375
- final_gain: float32 [5120], replicated, may hold values from 0.5 to 1.5
- final_weight: bfloat16 [5120, 64], P('seq'), may hold values from -0.078125 to 0.078125
- guide_stream: bfloat16 [6144, 2048], P('seq', 'head'), may hold values from -57 to 57
- guide_normed: bfloat16 [6144, 2048], P('seq', 'head'), may hold values from -41 to 41
- guide_qkv: bfloat16 [2048, 3, 1024], P('seq', None, 'head'), may hold values from -0.125 to 0.125
- guide_out: bfloat16 [1024, 2048], P('head', 'seq'), may hold values from -0.1875 to 0.1875
- guide_gain: float32 [2048], replicated, may hold values from 0.5 to 1.5
- guide_final: bfloat16 [2048, 64], P('seq'), may hold values from -0.125 to 0.125
- layout: int32 [6144], replicated, may hold values from 0 to 6143, each once
- flags: int32 [12], replicated, may hold values 0 or 1
Outputs:
- guided: float32 [6144, 64], P('seq')
Inputs may be any that keep to these rules, and one draw needn't show every extreme that they name: `layout`: each token appears in exactly one slot.
All inputs are finite; a program needn't handle non-finite values.
Results may differ from a plain program's by a relative error of at most 0.02.
The roundings to bfloat16 on the way count: a program that leaves them out, or rounds other values in their place, can miss the bound.
Values may be sent and summed in bfloat16 or wider, within the bound.
A program may use at most 128 MiB of HBM per device.

v0:
```python
import math

import jax
import jax.numpy as jnp
from jax import lax
from jax.sharding import PartitionSpec as P

HD = 128
FRAME_TOK = 512


EPS = 1e-05
TEMPER = 2.5


def project(inputs, weights):
    row_count, width = inputs.shape
    head_count = weights.shape[2] // HD
    packed = jnp.dot(
        inputs, weights.reshape(width, 3 * head_count * HD), preferred_element_type=jnp.float32
    )
    packed = packed.astype(jnp.bfloat16).reshape(row_count, 3, head_count * HD)
    queries = packed[:, 0].reshape(row_count, head_count, HD)
    return (queries, packed[:, 1], packed[:, 2])


def initial(queries):
    row_count, head_count, _ = queries.shape
    return (
        jnp.full((row_count, head_count), -1e30, jnp.float32),
        jnp.zeros((row_count, head_count), jnp.float32),
        jnp.zeros((row_count, head_count, HD), jnp.float32),
    )


def absorb(carried, queries, keys, values):
    head_count = queries.shape[1]
    key_rows = keys.shape[0]
    keys = keys.reshape(key_rows, head_count, HD)
    values = values.reshape(key_rows, head_count, HD)
    scores = jnp.einsum("qhd,khd->qhk", queries, keys, preferred_element_type=jnp.float32) * (
        TEMPER / math.sqrt(HD)
    )
    highest, totals, accum = carried
    new_high = jnp.maximum(highest, jnp.max(scores, axis=2))
    shrink = jnp.exp(highest - new_high)
    expd = jnp.exp(scores - new_high[:, :, None])
    totals = totals * shrink + jnp.sum(expd, axis=2)
    accum = accum * shrink[:, :, None] + jnp.einsum(
        "qhk,khd->qhd", expd.astype(jnp.bfloat16), values, preferred_element_type=jnp.float32
    )
    return (new_high, totals, accum)


def block_length(key_rows):
    length = min(key_rows, 1024)
    while key_rows % length:
        length -= 1
    return length


def blocked(advance, carried, pieces):
    key_rows = pieces[0].shape[0]
    length = block_length(key_rows)
    stacked = tuple(
        (item.reshape((key_rows // length, length) + item.shape[1:]) for item in pieces)
    )

    def scan_step(inner, blocks):
        return (advance(inner, blocks), None)

    carried, _ = lax.scan(scan_step, carried, stacked)
    return carried


def finish(carried):
    _, totals, accum = carried
    mixed = (accum / totals[:, :, None]).astype(jnp.bfloat16)
    return mixed.reshape(mixed.shape[0], mixed.shape[1] * HD)


def norm_rows(hidden, gains):
    center = jnp.mean(hidden, axis=1, keepdims=True)
    square = jnp.mean(hidden * hidden, axis=1, keepdims=True)
    spread = square - center * center
    return ((hidden - center) * lax.rsqrt(spread + EPS) * gains).astype(jnp.bfloat16)


def with_stream(partial_rows, shard, position):
    width = shard.shape[1]
    column = position * width
    placed = lax.dynamic_slice_in_dim(partial_rows, column, width, 1) + shard.astype(jnp.float32)
    return lax.dynamic_update_slice_in_dim(partial_rows, placed, column, 1)


def per_device(
    stream,
    normed,
    qkv_weight,
    out_weight,
    final_gain,
    final_weight,
    guide_stream,
    guide_normed,
    guide_qkv,
    guide_out,
    guide_gain,
    guide_final,
    layout,
    flags,
):
    row_count = normed.shape[0]
    full_in, guide_in = (
        lax.all_gather(normed, "head", axis=1, tiled=True),
        lax.all_gather(guide_normed, "head", axis=1, tiled=True),
    )
    out_whole, gqkv_whole, gout_whole, final_whole, gfinal_whole = (
        lax.all_gather(out_weight, "seq", axis=1, tiled=True),
        lax.all_gather(guide_qkv, "seq", axis=0, tiled=True),
        lax.all_gather(guide_out, "seq", axis=1, tiled=True),
        lax.all_gather(final_weight, "seq", axis=0, tiled=True),
        lax.all_gather(guide_final, "seq", axis=0, tiled=True),
    )
    main_query, main_key, main_value = project(full_in, qkv_weight)
    guide_query, guide_key, guide_value = project(guide_in, gqkv_whole)

    def absorb_both(carried, pieces):

        def advance(inner, blocks):
            return (
                absorb(inner[0], main_query, blocks[0], blocks[1]),
                absorb(inner[1], guide_query, blocks[2], blocks[3]),
            )

        return blocked(advance, carried, pieces)

    main_state, guide_state = absorb_both(
        (initial(main_query), initial(guide_query)),
        (
            lax.all_gather(main_key, "seq", axis=0, tiled=True),
            lax.all_gather(main_value, "seq", axis=0, tiled=True),
            lax.all_gather(guide_key, "seq", axis=0, tiled=True),
            lax.all_gather(guide_value, "seq", axis=0, tiled=True),
        ),
    )
    main_attn = finish(main_state)
    guide_attn = finish(guide_state)
    position = lax.axis_index("head")
    main_part = jnp.dot(main_attn, out_whole, preferred_element_type=jnp.float32)
    guide_part = jnp.dot(guide_attn, gout_whole, preferred_element_type=jnp.float32)
    main_hidden, guide_hidden = (
        lax.psum(with_stream(main_part, stream, position).astype(jnp.bfloat16), "head").astype(
            jnp.float32
        ),
        lax.psum(
            with_stream(guide_part, guide_stream, position).astype(jnp.bfloat16), "head"
        ).astype(jnp.float32),
    )
    main_pred = jnp.dot(
        norm_rows(main_hidden, final_gain), final_whole, preferred_element_type=jnp.float32
    )
    guide_pred = jnp.dot(
        norm_rows(guide_hidden, guide_gain), gfinal_whole, preferred_element_type=jnp.float32
    )
    every_pred = lax.all_gather(guide_pred.astype(jnp.bfloat16), "seq", axis=0, tiled=True).astype(
        guide_pred.dtype
    )
    token_count = layout.shape[0]
    inverse = (
        jnp.zeros((token_count,), jnp.int32)
        .at[layout]
        .set(jnp.arange(token_count, dtype=jnp.int32))
    )
    first_token = lax.axis_index("seq") * row_count
    slots = lax.dynamic_slice_in_dim(inverse, first_token, row_count)
    guide_mine = jnp.take(every_pred, slots, axis=0)
    owned = first_token + jnp.arange(row_count, dtype=jnp.int32)
    frame_ids = owned // FRAME_TOK
    frame_count = flags.shape[0]
    lookup = frame_ids[:, None] == jnp.arange(frame_count, dtype=jnp.int32)[None, :]
    strength = 1.0 + jnp.sum(jnp.where(lookup, flags[None, :], 0), axis=1).astype(jnp.float32)
    return guide_mine + strength[:, None] * (main_pred - guide_mine)


def solution(mesh):
    placed = (
        P("seq", "head"),
        P("seq", "head"),
        P(None, None, "head"),
        P("head", "seq"),
        P(),
        P("seq", None),
        P("seq", "head"),
        P("seq", "head"),
        P("seq", None, "head"),
        P("head", "seq"),
        P(),
        P("seq", None),
        P(),
        P(),
    )
    return jax.shard_map(
        per_device, mesh=mesh, in_specs=placed, out_specs=P("seq", None), check_vma=False
    )
```

profile of v0, /device:TPU:1, one launch (start us, length us, event | category | flops | bytes accessed | tf_op | source)
XLA Modules:
  0.0 809.4 jit_solution(12664361473143631664)
XLA Ops:
  8.1 56.8 %all_gather.39 = bf16[192,2048]{1,0:T(8,128)(2,1)S(1)} all-gather(bf16[192,256]{1,0:T(8,128)(2,1)} %param.23), channel_id=1, replica_groups=mesh['seq'=32,'head'=8] {'head'}, dimensions={1}, use_global_device_ids=true | all-gather | bytes 884736 | tf_op jit(solution)/shard_map/all_gather | solution.py:115
  64.8 21.5 %all-gather.16.cloned.1.call-done = bf16[2048,3,128]{2,0,1:T(8,128)(2,1)} async-done(((bf16[64,3,128]{2,0,1:T(8,128)(2,1)}), bf16[2048,3,128]{2,0,1:T(8,128)(2,1)}) %all-gather.16.cloned.1.call-update) | async-done | bytes 1572880 | tf_op jit(solution)/shard_map/all_gather | solution.py:119
  86.4 1.7 copy.51
  90.4 16.4 %copy.48 = bf16[5120,3,384]{0,2,1:T(8,128)(2,1)} copy(bf16[5120,3,384]{2,0,1:T(8,128)(2,1)} %param.18) | data formatting | bytes 23592960 | tf_op args[2]
  106.9 53.2 %all-gather.14.cloned.1.call-done = bf16[192,5120]{1,0:T(8,128)(2,1)} async-done(((bf16[192,640]{1,0:T(8,128)(2,1)}), bf16[192,5120]{1,0:T(8,128)(2,1)}) %all-gather.14.cloned.1.call-update) | async-done | bytes 1966096 | tf_op jit(solution)/shard_map/all_gather | solution.py:114
  160.1 9.0 %convolution_convert_fusion = bf16[192,1152]{1,0:T(8,128)(2,1)S(1)} fusion(bf16[192,5120]{1,0:T(8,128)(2,1)} %all-gather.14.cloned.1.call-done, bf16[5120,1152]{0,1:T(8,128)(2,1)} %bitcast.140), kind=kOutput, calls=%fused_computation.50 | convolution fusion | flops 2265145344 | bytes 14204928 | tf_op jit(solution)/shard_map/dot_general | solution.py:19
  172.7 46.3 %all_gather.43 = bf16[128,2048]{0,1:T(8,128)(2,1)} all-gather(bf16[128,64]{0,1:T(8,128)(2,1)S(1)} %copy-done.11), channel_id=1, replica_groups=mesh['seq'=32,'head'=8] {'seq'}, dimensions={1}, use_global_device_ids=true | all-gather | bytes 540672 | tf_op jit(solution)/shard_map/all_gather | solution.py:120
  220.3 59.1 %all-gather.26.cloned.1.call-done = bf16[6144,1,128]{2,0,1:T(8,128)(2,1)} async-done(((bf16[192,1,128]{2,0,1:T(8,128)(2,1)}), bf16[6144,1,128]{2,0,1:T(8,128)(2,1)}) %all-gather.26.cloned.1.call-update) | async-done | bytes 1572880 | tf_op jit(solution)/shard_map/all_gather | solution.py:143
  279.4 64.6 %all-gather.20.cloned.1.call-done = bf16[6144,1,384]{2,0,1:T(8,128)(2,1)} async-done(((bf16[192,1,384]{2,0,1:T(8,128)(2,1)}), bf16[6144,1,384]{2,0,1:T(8,128)(2,1)}) %all-gather.20.cloned.1.call-update) | async-done | bytes 4718608 | tf_op jit(solution)/shard_map/all_gather | solution.py:140
  344.1 64.5 %all-gather.22.cloned.1.call-done = bf16[6144,1,384]{2,0,1:T(8,128)(2,1)} async-done(((bf16[192,1,384]{2,0,1:T(8,128)(2,1)}), bf16[6144,1,384]{2,0,1:T(8,128)(2,1)}) %all-gather.22.cloned.1.call-update) | async-done | bytes 4718608 | tf_op jit(solution)/shard_map/all_gather | solution.py:141
  408.6 71.1 %while.21 = (s32[]{:T(128)}, f32[192,3]{0,1:T(4,128)S(1)}, f32[192,3]{0,1:T(4,128)S(1)}, f32[192,3,128]{2,0,1:T(8,128)S(1)}, f32[192,1]{0,1:T(1,128)}, /*index=5...) while((s32[]{:T(128)}, f32[192,3]{0,1:T(4,128)S(1)}, ...), condition=%wide.region_6.7_spmd.clone, body=%wide.region_1.6_spmd.clone.sunk | while | flops 408850176 | bytes 22210856 | solution.py:72
  408.6 2.4 constant_dynamic-slice_fusion.3
  415.1 1.8 fusion.106
  420.4 2.4 constant_dynamic-slice_fusion.3
  426.9 1.8 fusion.106
  432.2 2.4 constant_dynamic-slice_fusion.3
  438.8 1.8 fusion.106
  444.1 2.5 constant_dynamic-slice_fusion.3
  450.6 1.8 fusion.106
  456.0 2.4 constant_dynamic-slice_fusion.3
  462.5 1.8 fusion.106
  467.8 2.4 constant_dynamic-slice_fusion.3
  474.3 1.8 fusion.106
  479.6 3.7 fusion.59
  486.6 64.2 %all-gather.5 = bf16[32,160,64]{1,2,0:T(8,128)(2,1)S(1)} all-gather(bf16[1,160,64]{1,2,0:T(8,128)(2,1)S(1)} %bitcast.153), channel_id=1, replica_groups=mesh['seq'=32,'head'=8] {'seq'}, dimensions={0}, use_global_device_ids=true | all-gather | bytes 675840 | tf_op jit(solution)/shard_map/all_gather | solution.py:121
  551.4 2.5 reshape.180
  553.9 23.0 %scatter_custom_fusion = s32[6144]{0:T(1024)S(1)} fusion(s32[6144]{0:T(1024)S(1)} %compare_select_fusion, s32[6144]{0:T(1024)S(1)} %iota.12, s32[]{:T(128)} %constant.38.clone.1), kind=kCustom, calls=%fused_computation.86 | custom fusion | bytes 24580 | tf_op jit(solution)/shard_map/scatter | solution.py:172
  577.2 118.5 %all_gather.44 = bf16[2048,64]{1,0:T(8,128)(2,1)S(1)} all-gather(bf16[64,64]{1,0:T(8,128)(2,1)S(1)} %copy-done.12), channel_id=1, replica_groups=mesh['seq'=32,'head'=8] {'seq'}, dimensions={0}, use_global_device_ids=true | all-gather | bytes 270336 | tf_op jit(solution)/shard_map/all_gather | solution.py:122
  695.7 40.2 %all-reduce.3.cloned.1.call-done = (bf16[192,2048]{1,0:T(8,128)(2,1)}, bf16[192,5120]{1,0:T(8,128)(2,1)}) async-done(((bf16[192,2048]{1,0:T(8,128)(2,1)}, bf16[192,5120]{1,0:T(8,128)(2,1)}), (bf16[192,2048]{1,0:T(8,128)(2,1)}, bf16[192,5120]{1,0:T(8,128)(2,1)})) %all-reduce.3.cloned.1.call-update) | async-done | bytes 2752528 | tf_op jit(solution)/shard_map/psum | solution.py:155
  739.1 55.5 %all-gather.4 = bf16[32,192,64]{1,2,0:T(8,128)(2,1)} all-gather(bf16[1,192,64]{1,2,0:T(8,128)(2,1)S(1)} %fusion.54), channel_id=1, replica_groups=mesh['seq'=32,'head'=8] {'seq'}, dimensions={0}, use_global_device_ids=true | all-gather | bytes 811008 | tf_op jit(solution)/shard_map/all_gather | solution.py:165
  797.0 2.3 convert_reduce_fusion
  799.3 3.2 fusion.51
  (215 shorter events, 63.2 us)
Async XLA Ops:
  6.5 79.8 %all-gather.16.cloned.1.call-start = ((), (), s32[]{:S(2)}) async-start(), calls=%async_computation.1 | async-start | bytes 1622016 | tf_op jit(solution)/shard_map/all_gather | solution.py:119
  7.3 152.8 %all-gather.14.cloned.1.call-start = ((), (), s32[]{:S(2)}) async-start(), calls=%async_computation | async-start | bytes 2211840 | tf_op jit(solution)/shard_map/all_gather | solution.py:114
  8.0 212.3 %all-gather.24.cloned.1.call-start = ((), (), s32[]{:S(2)}) async-start(), calls=%async_computation.5 | async-start | bytes 1622016 | tf_op jit(solution)/shard_map/all_gather | solution.py:142
  89.7 189.8 %all-gather.26.cloned.1.call-start = ((), (), s32[]{:S(2)}) async-start(), calls=%async_computation.6 | async-start | bytes 1622016 | tf_op jit(solution)/shard_map/all_gather | solution.py:143
  90.4 253.7 %all-gather.20.cloned.1.call-start = ((), (), s32[]{:S(2)}) async-start(), calls=%async_computation.3 | async-start | bytes 4866048 | tf_op jit(solution)/shard_map/all_gather | solution.py:140
  169.0 3.7 copy-start.11
  171.1 237.5 %all-gather.22.cloned.1.call-start = ((), (), s32[]{:S(2)}) async-start(), calls=%async_computation.4 | async-start | bytes 4866048 | tf_op jit(solution)/shard_map/all_gather | solution.py:141
  171.8 307.8 %all-gather.18.cloned.1.call-start = ((), (), s32[]{:S(2)}) async-start(), calls=%async_computation.2 | async-start | bytes 4055040 | tf_op jit(solution)/shard_map/all_gather | solution.py:118
  172.6 563.3 %all-reduce.3.cloned.1.call-start = ((), (), s32[]{:S(2)}) async-start(), calls=%async_computation.7 | async-start | bytes 5505024 | tf_op jit(solution)/shard_map/psum | solution.py:155
  415.1 3.1 copy-start.4
  415.1 3.4 copy-start.6
  418.6 1.8 copy-start.7
  426.9 3.1 copy-start.4
  426.9 3.4 copy-start.6
  438.8 3.1 copy-start.4
  438.8 3.4 copy-start.6
  442.2 1.8 copy-start.7
  450.6 3.2 copy-start.4
  450.6 3.5 copy-start.6
  454.1 1.8 copy-start.7
  462.5 3.1 copy-start.4
  462.5 3.4 copy-start.6
  474.3 3.1 copy-start.4
  474.3 3.4 copy-start.6
  477.8 1.9 copy-start.7
  479.6 3.7 copy-start.3
  483.5 1.9 copy-start.5
  486.5 67.3 %copy-start.10 = (s32[6144]{0:T(1024)S(1)}, s32[6144]{0:T(1024)}, u32[]{:S(2)}) copy-start(s32[6144]{0:T(1024)} %param.28) | copy-start | bytes 73732
  486.6 90.5 %copy-start.13 = (s32[12]{0:T(128)S(1)}, s32[12]{0:T(128)}, u32[]{:S(2)}) copy-start(s32[12]{0:T(128)} %param.29) | copy-start | bytes 148
  486.6 90.6 %copy-start.12 = (bf16[64,64]{1,0:T(8,128)(2,1)S(1)}, bf16[64,64]{1,0:T(8,128)(2,1)}, u32[]{:S(2)}) copy-start(bf16[64,64]{1,0:T(8,128)(2,1)} %param.27) | copy-start | bytes 24580
  550.8 186.6 %copy-start.15 = (f32[2048]{0:T(1024)S(1)}, f32[2048]{0:T(1024)}, u32[]{:S(2)}) copy-start(f32[2048]{0:T(1024)} %param.26) | copy-start | bytes 24580
  796.2 3.1 copy-start.14
  (17 other events, 25.6 us)
Sparse Core Ops, SparseCore 0:
  9.2 77.0 all-gather.15
  89.0 71.0 all-gather.13
  161.9 57.2 all-gather.23
  220.9 58.4 all-gather.25
  281.1 62.8 all-gather.19
  345.8 62.7 all-gather.21
  410.4 61.4 all-gather.17
  486.7 249.1 all-reduce.2
where the time goes:
time: 811 us; the launch traced here: 809 us
  blocking collectives  341 us (42%)
  waiting for transfers between devices  305 us (38%)
  local copies, waits for them, and re-layouts  82.3 us (10%)
  matrix products  53.8 us (7%)
  between operations  13.8 us (2%)
  other arithmetic  12 us (1%)
    all_gather x1, blocking collectives, per_device(): lax.all_gather(guide_final, 'seq', axis=0, tiled=True)  119 us
    all_gather x1, waiting for transfers between devices, per_device(): lax.all_gather(main_key, 'seq', axis=0, tiled=True)  64.6 us
    all_gather x1, waiting for transfers between devices, per_device(): lax.all_gather(main_value, 'seq', axis=0, tiled=True)  64.5 us
    all_gather x1, blocking collectives, per_device(): lax.all_gather(final_weight, 'seq', axis=0, tiled=True)  64.2 us
    all_gather x1, waiting for transfers between devices, per_device(): lax.all_gather(guide_value, 'seq', axis=0, tiled=True)  59.1 us
    all_gather x1, blocking collectives, per_device(): lax.all_gather(guide_normed, 'head', axis=1, tiled=True)  56.8 us
    all_gather x1, blocking collectives, per_device(): lax.all_gather(guide_pred.astype(jnp.bfloat16), 'seq', axis=0, tiled=True)  55.5 us
    all_gather x1, waiting for transfers between devices, per_device(): lax.all_gather(normed, 'head', axis=1, tiled=True)  53.2 us
  transfers between devices with their start and end apart: 8, of which 6 were waited for; matrix products, arithmetic and copies ran while one was open for 16% of the time, Pallas kernels for 0%

commit v1 on v0

v1 whole, which is shorter than its diff:
```python
import math

import jax
import jax.numpy as jnp
from jax import lax
from jax.experimental import pallas as pl
from jax.experimental.pallas import tpu as pltpu
from jax.sharding import PartitionSpec as P

HD = 128
FRAME_TOK = 512
EPS = 1e-05
TEMPER = 2.5
SCALE2 = TEMPER / math.sqrt(HD) * math.log2(math.e)
F32, BF16 = jnp.float32, jnp.bfloat16
MESH = pl.DeviceIdType.MESH

ROWS = 192
HALF = 96
KC, GKC = 640, 256
TOKENS = 6144
QT = 256
NT = (((1,), (1,)), ((), ()))
TN = (((0,), (0,)), ((), ()))


def body(
    stream, normed, qkv_t, out_t, gain, fin, gstream, gnormed, gqkv_t, gout_t, ggain, gfin,
    layout, flags, out,
    xn, gn, qw, gq, wt, gwt, fw, gfw, sb, gsb, acc, gacc, packed, qb, kv, top, tot, ot, ob, at,
    hot, hid, ghid, sg, sm, pg, pm, rg, rm, gp, outb,
    send_sem, recv_sem, local_sem,
):
    s, g = lax.axis_index("seq"), lax.axis_index("head")
    y, zl, c = s // 8, (s // 2) % 4, s % 2
    x, zh = g // 2, g % 2

    def seq_of(yy, zz, cc):
        return yy * 8 + zz * 2 + cc

    def head_of(xx, hh):
        return xx * 2 + hh

    xp, xm, x2 = (x + 1) % 4, (x + 3) % 4, (x + 2) % 4
    yp, ym, y2 = (y + 1) % 4, (y + 3) % 4, (y + 2) % 4
    oc, oh = 1 - c, 1 - zh
    started = []
    count = [0]

    def role():
        count[0] += 1
        return count[0] - 1

    def copy(r, src, dst, ss, gg):
        return pltpu.make_async_remote_copy(
            src_ref=src, dst_ref=dst, send_sem=send_sem.at[r], recv_sem=recv_sem.at[r],
            device_id=(ss, gg), device_id_type=MESH,
        )

    def send(r, src, dst, ss, gg):
        one = copy(r, src, dst, ss, gg)
        one.start()
        started.append(one)

    def wait(r, dst):
        copy(r, dst, dst, seq_of(y, zl, oc), g).wait_recv()

    part_s, part_g = g * 4 + s % 4, s // 4
    same = jnp.logical_and(x == y, zh == zl // 2)
    barrier = pltpu.get_barrier_semaphore()
    peers = [(seq_of(y, (zl + d) % 4, c), g) for d in (1, 2, 3)]
    peers += [(seq_of(y, (zl + d) % 4, c), head_of(x, oh)) for d in (0, 1, 2, 3)]
    peers += [(s, head_of((x + d) % 4, h)) for d in (1, 2, 3) for h in (zh, oh)]
    peers += [(seq_of((y + d) % 4, zl, c), g) for d in (1, 2, 3)]
    peers += [(seq_of(y, zl, oc), g)]
    for ss, gg in peers:
        pl.semaphore_signal(barrier, inc=1, device_id=(ss, gg), device_id_type=MESH)

    @pl.when(jnp.logical_not(same))
    def _():
        pl.semaphore_signal(barrier, inc=1, device_id=(part_s, part_g), device_id_type=MESH)

    local = [
        (normed, xn.at[g]), (gnormed, gn.at[g]), (gqkv_t, gq.at[:, y, zl, c]),
        (qkv_t, qw), (stream, sb), (gstream, gsb),
    ]
    local = [pltpu.make_async_copy(a, b, local_sem.at[i]) for i, (a, b) in enumerate(local)]
    for one in local:
        one.start()

    pl.semaphore_wait(barrier, len(peers) + 1 - same.astype(jnp.int32))

    sets = [(xn, normed), (gn, gnormed)]
    r_cross = [role(), role()]
    r_p, r_m = [[role(), role()] for _ in sets], [[role(), role()] for _ in sets]
    r_rp, r_rm = [[role(), role()] for _ in sets], [[role(), role()] for _ in sets]
    for i, (buf, src) in enumerate(sets):
        send(r_cross[i], src, buf.at[g], s, head_of(x, oh))
    for i, (buf, src) in enumerate(sets):
        send(r_p[i][0], src, buf.at[g], s, head_of(xp, zh))
        send(r_m[i][0], src, buf.at[g], s, head_of(xm, zh))
    r_gqz = [role() for _ in range(3)]
    for d in (1, 2, 3):
        send(r_gqz[d - 1], gqkv_t, gq.at[:, y, zl, c], seq_of(y, (zl + d) % 4, c), g)

    moved = [
        (out_t, wt.at[x, zh * 2 + zl % 2, c], wt.at[y, zl, c]),
        (gout_t, gwt.at[x, zh * 2 + zl % 2, c], gwt.at[y, zl, c]),
        (fin, fw.at[zl % 2, c], fw.at[zl % 2, c]),
        (gfin, gfw.at[zl % 2, c], gfw.at[zl % 2, c]),
    ]
    r_perm = [role() for _ in moved]

    @pl.when(jnp.logical_not(same))
    def _():
        for r, (src, there, _) in zip(r_perm, moved):
            copy(r, src, there, part_s, part_g).start()

    @pl.when(same)
    def _():
        for r, (src, _, here) in zip(r_perm, moved):
            pltpu.make_async_copy(src, here, recv_sem.at[r]).start()

    token = s * ROWS + lax.broadcasted_iota(jnp.int32, (ROWS, 128), 0)
    for r in range(TOKENS // 128):
        row = layout[pl.ds(r, 1), :]
        hot[:, r * 128 : (r + 1) * 128] = jnp.where(token == row, 1.0, 0.0).astype(BF16)

    def relay(i, h):
        buf = sets[i][0]
        k = 0 if h is zh else 1
        from_m, from_p = head_of(xm, h), head_of(xp, h)
        wait(r_p[i][k], buf.at[from_m])
        send(r_rp[i][k], buf.at[from_m, 0:HALF], buf.at[from_m, 0:HALF], s, head_of(xp, zh))
        wait(r_m[i][k], buf.at[from_p])
        send(r_rm[i][k], buf.at[from_p, HALF:], buf.at[from_p, HALF:], s, head_of(xm, zh))

    def far(i, h):
        buf = sets[i][0]
        k = 0 if h is zh else 1
        wait(r_rp[i][k], buf.at[head_of(x2, h), 0:HALF])
        wait(r_rm[i][k], buf.at[head_of(x2, h), HALF:])

    def project(gg, first=False):
        rows = xn[gg]
        for i in range(3):
            part = jnp.dot(
                rows, qw[i, pl.ds(pl.multiple_of(gg * KC, KC), KC), :], preferred_element_type=F32
            )
            acc[i] = part if first else acc[i] + part

    def gproject(gg, first=False):
        rows = gn[gg]
        for i in range(3):
            block = gq[i, gg // 2, pl.ds((gg % 2) * 2, 2)].reshape(GKC, HD)
            part = jnp.dot(rows, block, preferred_element_type=F32)
            gacc[i] = part if first else gacc[i] + part

    relay(0, zh)
    relay(1, zh)
    for i, (buf, _) in enumerate(sets):
        other = buf.at[head_of(x, oh)]
        wait(r_cross[i], other)
        send(r_p[i][1], other, other, s, head_of(xp, zh))
        send(r_m[i][1], other, other, s, head_of(xm, zh))
    local[2].wait()
    for d in (1, 2, 3):
        wait(r_gqz[d - 1], gq.at[:, y, (zl + 4 - d) % 4, c])
    r_gqp, r_gqm, r_gqrp, r_gqrm, r_gqc = role(), role(), role(), role(), role()
    mine = gq.at[:, y, :, c]
    send(r_gqp, mine, mine, seq_of(yp, zl, c), g)
    send(r_gqm, mine, mine, seq_of(ym, zl, c), g)
    for r, (_, _, here) in zip(r_perm, moved):
        wait(r, here)
    r_wz, r_gwz = [role() for _ in range(3)], [role() for _ in range(3)]
    for d in (1, 2, 3):
        there = seq_of(y, (zl + d) % 4, c)
        send(r_wz[d - 1], wt.at[y, zl, c], wt.at[y, zl, c], there, g)
        send(r_gwz[d - 1], gwt.at[y, zl, c], gwt.at[y, zl, c], there, g)
    zn = zl + 1 - 2 * (zl % 2)
    r_fz, r_gfz = role(), role()
    send(r_fz, fw.at[zl % 2, c], fw.at[zl % 2, c], seq_of(y, zn, c), g)
    send(r_gfz, gfw.at[zl % 2, c], gfw.at[zl % 2, c], seq_of(y, zn, c), g)

    for i in (0, 1, 3):
        local[i].wait()
    project(g, True)
    project(head_of(xm, zh))
    project(head_of(xp, zh))
    a, b = gq.at[:, ym, 0:2, c], gq.at[:, yp, 2:4, c]
    wait(r_gqp, gq.at[:, ym, :, c])
    send(r_gqrp, a, a, seq_of(yp, zl, c), g)
    wait(r_gqm, gq.at[:, yp, :, c])
    send(r_gqrm, b, b, seq_of(ym, zl, c), g)
    project(head_of(x, oh))
    relay(0, oh)
    relay(1, oh)
    far(0, zh)
    project(head_of(x2, zh))
    wait(r_gqrp, gq.at[:, y2, 0:2, c])
    wait(r_gqrm, gq.at[:, y2, 2:4, c])
    send(r_gqc, gq.at[:, :, :, c], gq.at[:, :, :, c], seq_of(y, zl, oc), g)
    project(head_of(xm, oh))
    project(head_of(xp, oh))
    wait(r_gqc, gq.at[:, :, :, oc])
    far(1, zh)
    gproject(g, True)
    for gg in (head_of(xm, zh), head_of(xp, zh), head_of(x2, zh), head_of(x, oh)):
        gproject(gg)
    gproject(head_of(xm, oh))
    gproject(head_of(xp, oh))
    far(0, oh)
    project(head_of(x2, oh))
    far(1, oh)
    gproject(head_of(x2, oh))
    for i in range(3):
        for j in range(3):
            packed[i, j] = acc[i, :, j * HD : (j + 1) * HD].astype(BF16)
        packed[i, 3] = gacc[i].astype(BF16)

    own = [
        pltpu.make_async_copy(packed.at[0, zl], qb.at[zl], local_sem.at[6]),
        pltpu.make_async_copy(packed.at[1:3, zl], kv.at[:, y, c, zl], local_sem.at[7]),
    ]
    for one in own:
        one.start()
    r_q, r_kv = [role() for _ in range(3)], [role() for _ in range(3)]
    for d in (1, 2, 3):
        j = (zl + d) % 4
        there = seq_of(y, j, c)
        send(r_kv[d - 1], packed.at[1:3, j], kv.at[:, y, c, zl], there, g)
    for d in (1, 2, 3):
        j = (zl + d) % 4
        send(r_q[d - 1], packed.at[0, j], qb.at[zl], seq_of(y, j, c), g)
    r_kp, r_km = [role() for _ in range(4)], [role() for _ in range(4)]
    r_kc, r_kr = [role() for _ in range(4)], [role() for _ in range(4)]
    r_kcm, r_kcp, r_kc2 = role(), role(), role()
    for d in range(4):
        k = (zl + 4 - d) % 4
        block = kv.at[:, y, c, k]
        if d == 0:
            own[1].wait()
        else:
            wait(r_kv[d - 1], block)
        send(r_kp[d], block, block, seq_of(yp, zl, c), g)
        send(r_km[d], block, block, seq_of(ym, zl, c), g)
        send(r_kc[d], block, block, seq_of(y, zl, oc), g)
    own[0].wait()
    for d in (1, 2, 3):
        wait(r_q[d - 1], qb.at[(zl + 4 - d) % 4])

    def absorb(yy, cc, first=False):
        keys = kv[0, yy, cc].reshape(4 * ROWS, HD)
        values = kv[1, yy, cc].reshape(4 * ROWS, HD)

        def tile(t, _):
            scores = lax.dot_general(
                keys, ob[pl.ds(pl.multiple_of(t * QT, QT), QT), :], NT, preferred_element_type=F32
            )
            highest = jnp.max(scores, axis=0, keepdims=True)
            if not first:
                before = top[t]
                highest = jnp.maximum(highest, before)
            expd = jnp.exp2((scores - highest) * SCALE2)
            total = jnp.sum(expd, axis=0, keepdims=True)
            mixed = lax.dot_general(values, expd.astype(BF16), TN, preferred_element_type=F32)
            top[t] = highest
            if first:
                tot[t] = total
                ot[t] = mixed
            else:
                shrink = jnp.exp2((before - highest) * SCALE2)
                tot[t] = tot[t] * shrink + total
                ot[t] = ot[t] * shrink + mixed
            return 0

        lax.fori_loop(0, 3, tile, 0)

    for k in range(4):
        ob[k * ROWS : (k + 1) * ROWS, :] = qb[k]
    absorb(y, c, True)
    for d in (0, 1):
        k = (zl + 4 - d) % 4
        wait(r_kp[d], kv.at[:, ym, c, k])
        send(r_kr[d], kv.at[:, ym, c, k], kv.at[:, ym, c, k], seq_of(yp, zl, c), g)
    for d in (2, 3):
        k = (zl + 4 - d) % 4
        wait(r_km[d], kv.at[:, yp, c, k])
        send(r_kr[d], kv.at[:, yp, c, k], kv.at[:, yp, c, k], seq_of(ym, zl, c), g)
    for d in range(4):
        wait(r_kc[d], kv.at[:, y, oc, (zl + 4 - d) % 4])
    absorb(y, oc)
    for d in (2, 3):
        wait(r_kp[d], kv.at[:, ym, c, (zl + 4 - d) % 4])
    send(r_kcm, kv.at[:, ym, c], kv.at[:, ym, c], seq_of(y, zl, oc), g)
    for d in (0, 1):
        wait(r_km[d], kv.at[:, yp, c, (zl + 4 - d) % 4])
    send(r_kcp, kv.at[:, yp, c], kv.at[:, yp, c], seq_of(y, zl, oc), g)
    for d in (1, 2, 3):
        wait(r_wz[d - 1], wt.at[y, (zl + 4 - d) % 4, c])
        wait(r_gwz[d - 1], gwt.at[y, (zl + 4 - d) % 4, c])
    r_w = [[role() for _ in range(6)] for _ in range(2)]
    for r, buf in zip(r_w, (wt, gwt)):
        block = buf.at[y, :, c]
        send(r[0], block, block, seq_of(yp, zl, c), g)
        send(r[1], block, block, seq_of(ym, zl, c), g)
    wait(r_fz, fw.at[1 - zl % 2, c])
    wait(r_gfz, gfw.at[1 - zl % 2, c])
    r_fc, r_gfc = role(), role()
    send(r_fc, fw.at[:, c], fw.at[:, c], seq_of(y, zl, oc), g)
    send(r_gfc, gfw.at[:, c], gfw.at[:, c], seq_of(y, zl, oc), g)
    absorb(ym, c)
    absorb(yp, c)
    for d in range(4):
        wait(r_kr[d], kv.at[:, y2, c, (zl + 4 - d) % 4])
    send(r_kc2, kv.at[:, y2, c], kv.at[:, y2, c], seq_of(y, zl, oc), g)
    wait(r_kcm, kv.at[:, ym, oc])
    absorb(ym, oc)
    wait(r_kcp, kv.at[:, yp, oc])
    absorb(yp, oc)
    absorb(y2, c)
    for r, buf in zip(r_w, (wt, gwt)):
        a, b = buf.at[ym, 0:2, c], buf.at[yp, 2:4, c]
        wait(r[0], buf.at[ym, :, c])
        send(r[2], a, a, seq_of(yp, zl, c), g)
        wait(r[1], buf.at[yp, :, c])
        send(r[3], b, b, seq_of(ym, zl, c), g)
    wait(r_kc2, kv.at[:, y2, oc])
    absorb(y2, oc)
    for t in range(3):
        done = (ot[t] / tot[t]).T.astype(BF16)
        ob[t * QT : (t + 1) * QT, :] = done

    r_o = [[role(), role()] for _ in range(4)]
    for d in (0, 1, 2, 3):
        k = (zl + d) % 4
        block = ob.at[pl.ds(pl.multiple_of(k * ROWS, ROWS), ROWS), :]
        for e, h in enumerate((zh, oh)):
            if d == 0 and e == 0:
                pltpu.make_async_copy(block, at.at[x, zh, zl], recv_sem.at[r_o[0][0]]).start()
            else:
                send(r_o[d][e], block, at.at[x, zh, zl], seq_of(y, k, c), head_of(x, h))
    first_o = r_o[0][0]

    def arrived(j):
        d = (zl + 4 - j) % 4
        for e, h in enumerate((zh, oh)):
            wait(first_o + d * 2 + e, at.at[x, h, j])

    r_gx = [role() for _ in range(4)]
    r_mx = [role() for _ in range(4)]
    arrived(3)
    send(r_gx[0], at.at[x, :, 3], at.at[x, :, 3], s, head_of(xp, zh))
    send(r_gx[1], at.at[x, :, 3], at.at[x, :, 3], s, head_of(xm, zh))
    for j in range(3):
        arrived(j)
    send(r_mx[0], at.at[x, :, 0:3], at.at[x, :, 0:3], s, head_of(xp, zh))
    send(r_mx[1], at.at[x, :, 0:3], at.at[x, :, 0:3], s, head_of(xm, zh))

    for r, buf in zip(r_w, (wt, gwt)):
        wait(r[2], buf.at[y2, 0:2, c])
        wait(r[3], buf.at[y2, 2:4, c])
        send(r[4], buf.at[:, :, c], buf.at[:, :, c], seq_of(y, zl, oc), g)
    wait(r_gx[0], at.at[xm, :, 3])
    send(r_gx[2], at.at[xm, 0, 3], at.at[xm, 0, 3], s, head_of(xp, zh))
    wait(r_gx[1], at.at[xp, :, 3])
    send(r_gx[3], at.at[xp, 1, 3], at.at[xp, 1, 3], s, head_of(xm, zh))
    local[4].wait()
    local[5].wait()
    wait(r_w[1][4], gwt.at[:, :, oc])

    def gout_part(xx):
        total = None
        for h in range(2):
            block = gwt[xx, h * 2 : h * 2 + 2].reshape(GKC, HD)
            part = lax.dot_general(at[xx, h, 3], block, NT, preferred_element_type=F32)
            total = part if total is None else total + part
        return total

    def out_part(xx):
        total = None
        for h in range(2):
            rows = jnp.concatenate([at[xx, h, j] for j in range(3)], axis=1)
            block = wt[xx, h * 2 : h * 2 + 2].reshape(KC, 3 * HD)
            part = lax.dot_general(rows, block, NT, preferred_element_type=F32)
            total = part if total is None else total + part
        return total

    ghid[...] = gsb[...].astype(F32) + gout_part(x)
    ghid[...] += gout_part(xm)
    ghid[...] += gout_part(xp)
    wait(r_w[0][4], wt.at[:, :, oc])
    hid[...] = sb[...].astype(F32) + out_part(x)
    wait(r_mx[0], at.at[xm, :, 0:3])
    send(r_mx[2], at.at[xm, 0, 0:3], at.at[xm, 0, 0:3], s, head_of(xp, zh))
    wait(r_mx[1], at.at[xp, :, 0:3])
    send(r_mx[3], at.at[xp, 1, 0:3], at.at[xp, 1, 0:3], s, head_of(xm, zh))
    wait(r_gx[2], at.at[x2, 0, 3])
    wait(r_gx[3], at.at[x2, 1, 3])
    ghid[...] += gout_part(x2)

    def spread_stats(buf, ref, width, roles):
        one = jnp.zeros((ROWS, 128), F32)
        two = jnp.zeros((ROWS, 128), F32)
        for i in range(width // 128):
            cols = ref[:, i * 128 : (i + 1) * 128]
            one = one + cols
            two = two + cols * cols
        buf[g, 0:1, :] = jnp.sum(one.T, axis=0, keepdims=True)
        buf[g, 1:2, :] = jnp.sum(two.T, axis=0, keepdims=True)
        buf[g, 2:8, :] = jnp.zeros((6, ROWS), F32)
        for d in range(1, 8):
            send(roles[d - 1], buf.at[g], buf.at[g], s, (g + d) % 8)

    def gather_stats(buf, width, roles):
        for d in range(1, 8):
            wait(roles[d - 1], buf.at[(g + 8 - d) % 8])
        sums = buf[0]
        for i in range(1, 8):
            sums = sums + buf[i]
        sums = sums * (1.0 / width)
        center = sums[0:1]
        scale = lax.rsqrt(sums[1:2] - center * center + EPS)
        return jnp.broadcast_to(center, (128, ROWS)).T, jnp.broadcast_to(scale, (128, ROWS)).T

    def predict(ref, width, center, scale, gains, weights):
        parts = []
        for i in range(width // 128):
            row = gains[pl.ds(g * (width // 128) + i, 1), :]
            cols = ref[:, i * 128 : (i + 1) * 128]
            parts.append(((cols - center) * scale * row).astype(BF16))
        normal = jnp.concatenate(parts, axis=1)
        return jnp.dot(normal, weights[...].reshape(width, 64), preferred_element_type=F32).T

    def spread_pred(pred, keep, buf, roles):
        for i in range(8):
            keep[i] = pred[i * 8 : (i + 1) * 8]
        for d in range(1, 8):
            k = (g + d) % 8
            send(roles[d - 1], keep.at[k], buf.at[g], s, k)
        buf[g] = keep[g]

    def gather_pred(buf, roles):
        for d in range(1, 8):
            wait(roles[d - 1], buf.at[(g + 8 - d) % 8])
        total = buf[0]
        for i in range(1, 8):
            total = total + buf[i]
        return total

    r_sg, r_sm, r_pg, r_pm, r_out = ([role() for _ in range(7)] for _ in range(5))
    spread_stats(sg, ghid, GKC, r_sg)
    hid[...] += out_part(xm)
    wait(r_fc, fw.at[:, oc])
    wait(r_gfc, gfw.at[:, oc])
    center, scale = gather_stats(sg, 2048, r_sg)
    spread_pred(predict(ghid, GKC, center, scale, ggain, gfw), pg, rg, r_pg)
    hid[...] += out_part(xp)
    gp[y, zl, c] = gather_pred(rg, r_pg)
    r_az, r_ay, r_ac = [role() for _ in range(3)], [role() for _ in range(3)], role()
    for d in (1, 2, 3):
        block = gp.at[y, zl, c]
        send(r_az[d - 1], block, block, seq_of(y, (zl + d) % 4, c), g)
    wait(r_mx[2], at.at[x2, 0, 0:3])
    wait(r_mx[3], at.at[x2, 1, 0:3])
    hid[...] += out_part(x2)
    spread_stats(sm, hid, KC, r_sm)
    for d in (1, 2, 3):
        wait(r_az[d - 1], gp.at[y, (zl + 4 - d) % 4, c])
    for d in (1, 2, 3):
        block = gp.at[y, :, c]
        send(r_ay[d - 1], block, block, seq_of((y + d) % 4, zl, c), g)
    center, scale = gather_stats(sm, 5120, r_sm)
    spread_pred(predict(hid, KC, center, scale, gain, fw), pm, rm, r_pm)
    for d in (1, 2, 3):
        wait(r_ay[d - 1], gp.at[(y + 4 - d) % 4, :, c])
    block = gp.at[:, :, c]
    send(r_ac, block, block, seq_of(y, zl, oc), g)
    wait(r_ac, gp.at[:, :, oc])

    lane = lax.broadcasted_iota(jnp.int32, (8, 128), 1)
    pieces = []
    for yy in range(4):
        for zz in range(4):
            a0, a1 = gp[yy, zz, 0, :, 0:128], gp[yy, zz, 0, :, 128:192]
            b0, b1 = gp[yy, zz, 1, :, 0:64], gp[yy, zz, 1, :, 64:192]
            pieces += [a0, jnp.concatenate([a1, b0], axis=1), b1]
    slots = jnp.concatenate(pieces, axis=1)
    high = slots.astype(BF16)
    low = (slots - high.astype(F32)).astype(BF16)
    picked = lax.dot_general(high, hot[...], NT, preferred_element_type=F32)
    picked = picked + lax.dot_general(low, hot[...], NT, preferred_element_type=F32)

    first = s * ROWS
    frame = first // FRAME_TOK
    last = (first + ROWS - 1) // FRAME_TOK
    owned = first + lax.broadcasted_iota(jnp.int32, (8, ROWS), 1)
    strength = 1.0 + jnp.where(owned // FRAME_TOK == frame, flags[frame], flags[last]).astype(F32)
    outb[g] = picked + strength * (gather_pred(rm, r_pm) - picked)
    for d in range(1, 8):
        send(r_out[d - 1], outb.at[g], outb.at[g], s, (g + d) % 8)
    for d in range(1, 8):
        wait(r_out[d - 1], outb.at[(g + 8 - d) % 8])
    for i in range(8):
        out[i * 8 : (i + 1) * 8, :] = outb[i]

    for one in started:
        one.wait_send()

    @pl.when(jnp.logical_not(same))
    def _():
        for r, (src, there, _) in zip(r_perm, moved):
            copy(r, src, there, part_s, part_g).wait_send()


def per_device(
    stream, normed, qkv_weight, out_weight, final_gain, final_weight, guide_stream, guide_normed,
    guide_qkv, guide_out, guide_gain, guide_final, layout, flags,
):
    anyw = pl.BlockSpec(memory_space=pl.ANY)
    vmem = pl.BlockSpec(memory_space=pltpu.VMEM)
    smem = pl.BlockSpec(memory_space=pltpu.SMEM)
    v = pltpu.VMEM
    scratch = [
        v((8, ROWS, KC), BF16),
        v((8, ROWS, GKC), BF16),
        v((3, 5120, 384), BF16),
        v((3, 4, 4, 2, 64, HD), BF16),
        v((4, 4, 2, 160, 384), BF16),
        v((4, 4, 2, 64, HD), BF16),
        v((2, 2, 160, 64), BF16),
        v((2, 2, 64, 64), BF16),
        v((ROWS, KC), BF16),
        v((ROWS, GKC), BF16),
        v((3, ROWS, 384), F32),
        v((3, ROWS, HD), F32),
        v((3, 4, ROWS, HD), BF16),
        v((4, ROWS, HD), BF16),
        v((2, 4, 2, 4, ROWS, HD), BF16),
        v((3, 1, QT), F32),
        v((3, 1, QT), F32),
        v((3, HD, QT), F32),
        v((4 * ROWS, HD), BF16),
        v((4, 2, 4, ROWS, HD), BF16),
        v((ROWS, TOKENS), BF16),
        v((ROWS, KC), F32),
        v((ROWS, GKC), F32),
        v((8, 8, ROWS), F32),
        v((8, 8, ROWS), F32),
        v((8, 8, ROWS), F32),
        v((8, 8, ROWS), F32),
        v((8, 8, ROWS), F32),
        v((8, 8, ROWS), F32),
        v((4, 4, 2, 8, ROWS), F32),
        v((8, 8, ROWS), F32),
        pltpu.SemaphoreType.DMA((160,)),
        pltpu.SemaphoreType.DMA((160,)),
        pltpu.SemaphoreType.DMA((8,)),
    ]
    guided = pl.pallas_call(
        body,
        out_shape=jax.ShapeDtypeStruct((64, ROWS), F32),
        in_specs=[anyw] * 4 + [vmem] + [anyw] * 5 + [vmem, anyw, vmem, smem],
        out_specs=vmem,
        scratch_shapes=scratch,
        compiler_params=pltpu.CompilerParams(
            collective_id=0, has_side_effects=True, vmem_limit_bytes=56 * 1024 * 1024
        ),
        cost_estimate=pl.CostEstimate(
            flops=6_000_000_000, bytes_accessed=20_000_000, transcendentals=5_000_000
        ),
    )(
        stream, normed, jnp.transpose(qkv_weight, (1, 0, 2)), out_weight.T,
        final_gain.reshape(40, 128), final_weight, guide_stream, guide_normed,
        jnp.transpose(guide_qkv, (1, 0, 2)), guide_out.T, guide_gain.reshape(16, 128), guide_final,
        layout.reshape(48, 128), flags,
    )
    return guided.T


def solution(mesh):
    placed = (
        P("seq", "head"),
        P("seq", "head"),
        P(None, None, "head"),
        P("head", "seq"),
        P(),
        P("seq", None),
        P("seq", "head"),
        P("seq", "head"),
        P("seq", None, "head"),
        P("head", "seq"),
        P(),
        P("seq", None),
        P(),
        P(),
    )
    return jax.shard_map(
        per_device, mesh=mesh, in_specs=placed, out_specs=P("seq", None), check_vma=False
    )
```

time: 811 us -> 147 us (0.18)
  blocking collectives: 341 us -> 0 us
  waiting for transfers between devices: 305 us -> 0 us
  Pallas kernels: 0 us -> 143 us
  local copies, waits for them, and re-layouts: 82.3 us -> 2.95 us
  matrix products: 53.8 us -> 0 us
  between operations: 13.8 us -> 0.01 us
  other arithmetic: 12 us -> 0 us
    all_gather x5 -> x0, blocking collectives: 341 us -> none  [the longest x1 119 us: per_device(): lax.all_gather(guide_final, 'seq', axis=0, tiled=True)]
    all_gather x7 -> x0, waiting for transfers between devices: 263 us -> none  [the longest x1 64.6 us: per_device(): lax.all_gather(main_key, 'seq', axis=0, tiled=True)]
    pallas_call x0 -> x1, Pallas kernels: none -> 143 us  [per_device(): pl.pallas_call(body, out_shape=jax.ShapeDtypeStruct((64, ROWS), F32), in_...]
    dot_general x30 -> x0, matrix products: 53.8 us -> none  [the longest x12 18.5 us: absorb(): jnp.einsum('qhk,khd->qhd', expd.astype(jnp.bfloat16), values, preferred_e...]
    psum x1 -> x0, waiting for transfers between devices: 40.2 us -> none  [per_device(): lax.psum(with_stream(guide_part, guide_stream, position).astype(jnp.bfloa...]
    dynamic_slice x18 -> x0, local copies, waits for them, and re-layouts: 23.5 us -> none  [blocked(): carried, _ = lax.scan(scan_step, carried, stacked)]
    scatter x1 -> x0, local copies, waits for them, and re-layouts: 23 us -> none  [per_device(): inverse = jnp.zeros((token_count,), jnp.int32).at[layout].set(jnp.arange(...]
    unnamed x26 -> x2, local copies, waits for them, and re-layouts: 20.3 us -> 2.95 us
  transfers between devices with their start and end apart: 8 -> 0, of which waited for: 6 -> 0; matrix products, arithmetic and copies ran while one was open for 16% -> 0% of each run, Pallas kernels for 0% -> 0%
where the time goes in v1:
time: 147 us; the launch traced here: 146 us
  Pallas kernels  143 us (97%)
  local copies, waits for them, and re-layouts  2.95 us (2%)
    pallas_call x1, Pallas kernels, per_device(): pl.pallas_call(body, out_shape=jax.ShapeDtypeStruct((64, ROWS), F32), in_...  143 us
    unnamed x2, local copies, waits for them, and re-layouts  2.95 us

profile of v1, /device:TPU:1, one launch (start us, length us, event | category | flops | bytes accessed | tf_op | source)
XLA Modules:
  0.0 145.7 jit_solution(16930792387149307826)
XLA Ops:
  0.0 1.5 %copy.15.fin = bf16[160,64]{1,0:T(8,128)(2,1)} copy(bf16[160,64]{0,1:T(8,128)(2,1)} %param.19) | data formatting | bytes 40960 | tf_op args[5]
  1.5 142.7 %shard_map.136 = f32[64,192]{1,0:T(8,128)} custom-call(bf16[192,640]{1,0:T(8,128)(2,1)} %stream.1, bf16[192,640]{1,0:T(8,128)(2,1)} %normed.1, bf16[3,5120,384]{2,1,0:T(8,128)(2,1)} %bitcast.9, bf16[160,384]{1,0:T(8,128)(2,1)} %bitcast.10, f32[40,128]{1,0:T(8,128)} %bitcast.13, bf16[160,64]{1,0:T(8,128)(2,1)} %copy.15.fin, bf16[192,256]{1,0:T(8,128)(2,1)} %gstream.1, ...), custom_call_target="tpu_custom_call" | custom-call | flops 6000000000 | bytes 20000000 | tf_op jit(solution)/shard_map/pallas_call | solution.py:560
  144.2 1.5 %copy.17 = f32[192,64]{0,1:T(8,128)} copy(f32[192,64]{0,1:T(8,128)} %bitcast.8) | data formatting | bytes 98304

commit v2 on v1

v2 whole, which is shorter than its diff:
```python
import math

import jax
import jax.numpy as jnp
from jax import lax
from jax.experimental import pallas as pl
from jax.experimental.pallas import tpu as pltpu
from jax.sharding import PartitionSpec as P

HD = 128
FRAME_TOK = 512
EPS = 1e-05
TEMPER = 2.5
SCALE2 = TEMPER / math.sqrt(HD) * math.log2(math.e)
F32, BF16 = jnp.float32, jnp.bfloat16
MESH = pl.DeviceIdType.MESH

ROWS = 192
HALF = 96
KC, GKC = 640, 256
TOKENS = 6144
NT = (((1,), (1,)), ((), ()))
TN = (((0,), (0,)), ((), ()))


def body(
    stream, normed, qkv_t, out_t, gain, fin_t, gstream, gnormed, gqkv_t, gout_t, ggain, gfin,
    layout, flags, out,
    xn, gn, qw, gq, wt, gwt, fw, gfw, sb, gsb, acc, gacc, packed, qb, kv, top, tot, ot, ob, at,
    hot, hid, ghid, fin, pg, pm, rg, rm, gp, outb,
    send_sem, recv_sem, local_sem,
):
    s, g = lax.axis_index("seq"), lax.axis_index("head")
    y, zl, c = s // 8, (s // 2) % 4, s % 2
    x, zh = g // 2, g % 2

    def seq_of(yy, zz, cc):
        return yy * 8 + zz * 2 + cc

    def head_of(xx, hh):
        return xx * 2 + hh

    xp, xm, x2 = (x + 1) % 4, (x + 3) % 4, (x + 2) % 4
    yp, ym, y2 = (y + 1) % 4, (y + 3) % 4, (y + 2) % 4
    oc, oh = 1 - c, 1 - zh
    started = []
    count = [0]

    def role():
        count[0] += 1
        return count[0] - 1

    def copy(r, src, dst, ss, gg):
        return pltpu.make_async_remote_copy(
            src_ref=src, dst_ref=dst, send_sem=send_sem.at[r], recv_sem=recv_sem.at[r],
            device_id=(ss, gg), device_id_type=MESH,
        )

    def send(r, src, dst, ss, gg):
        one = copy(r, src, dst, ss, gg)
        one.start()
        started.append(one)

    def wait(r, dst):
        copy(r, dst, dst, seq_of(y, zl, oc), g).wait_recv()

    part_s, part_g = g * 4 + s % 4, s // 4
    same = jnp.logical_and(x == y, zh == zl // 2)
    barrier = pltpu.get_barrier_semaphore()
    peers = [(seq_of(y, (zl + d) % 4, c), g) for d in (1, 2, 3)]
    peers += [(seq_of(y, (zl + d) % 4, c), head_of(x, oh)) for d in (0, 1, 2, 3)]
    peers += [(s, head_of((x + d) % 4, h)) for d in (1, 2, 3) for h in (zh, oh)]
    peers += [(seq_of((y + d) % 4, zl, c), g) for d in (1, 2, 3)]
    peers += [(seq_of(y, (zl + d) % 4, oc), g) for d in (0, 1, 2, 3)]
    for ss, gg in peers:
        pl.semaphore_signal(barrier, inc=1, device_id=(ss, gg), device_id_type=MESH)

    @pl.when(jnp.logical_not(same))
    def _():
        pl.semaphore_signal(barrier, inc=1, device_id=(part_s, part_g), device_id_type=MESH)

    local = [
        (normed, xn.at[g]), (gnormed, gn.at[g]), (gqkv_t, gq.at[:, y, zl, c]),
        (qkv_t, qw), (stream, sb), (gstream, gsb),
    ]
    local = [pltpu.make_async_copy(a, b, local_sem.at[i]) for i, (a, b) in enumerate(local)]
    for one in local:
        one.start()

    token = s * ROWS + lax.broadcasted_iota(jnp.int32, (ROWS, 128), 0)
    for r in range(TOKENS // 128):
        row = layout[pl.ds(r, 1), :]
        hot[:, r * 128 : (r + 1) * 128] = jnp.where(token == row, 1.0, 0.0).astype(BF16)
    fin[...] = fin_t[...].astype(F32).T.astype(BF16)
    for buf in (pg, pm):
        buf[...] = jnp.zeros_like(buf)

    pl.semaphore_wait(barrier, len(peers) + 1 - same.astype(jnp.int32))

    r_gqz = [role() for _ in range(3)]
    for d in (1, 2, 3):
        send(r_gqz[d - 1], gqkv_t, gq.at[:, y, zl, c], seq_of(y, (zl + d) % 4, c), g)
    low, high = pl.ds(0, HALF), pl.ds(HALF, HALF)
    whole = pl.ds(0, ROWS)
    sets = [
        (gn, gnormed, whole, low, high), (xn, normed, low, low, None), (xn, normed, high, None, high),
    ]
    r_cross, r_p, r_m, r_rp, r_rm = (
        [[role(), role()] for _ in sets] for _ in range(5)
    )
    for i, (buf, src, rows, _, _) in enumerate(sets):
        send(r_cross[i][0], src.at[rows], buf.at[g, rows], s, head_of(x, oh))
    for i, (buf, src, rows, _, _) in enumerate(sets):
        send(r_p[i][0], src.at[rows], buf.at[g, rows], s, head_of(xp, zh))
        send(r_m[i][0], src.at[rows], buf.at[g, rows], s, head_of(xm, zh))

    moved = [
        (out_t, wt.at[x, zh * 2 + zl % 2, c], wt.at[y, zl, c]),
        (gout_t, gwt.at[x, zh * 2 + zl % 2, c], gwt.at[y, zl, c]),
        (fin, fw.at[zl % 2, c], fw.at[zl % 2, c]),
        (gfin, gfw.at[zl % 2, c], gfw.at[zl % 2, c]),
    ]
    r_perm = [role() for _ in moved]

    @pl.when(jnp.logical_not(same))
    def _():
        for r, (src, there, _) in zip(r_perm, moved):
            copy(r, src, there, part_s, part_g).start()

    @pl.when(same)
    def _():
        for r, (src, _, here) in zip(r_perm, moved):
            pltpu.make_async_copy(src, here, recv_sem.at[r]).start()

    def relay(i, h):
        buf, _, rows, up, down = sets[i]
        k = 0 if h is zh else 1
        from_m, from_p = head_of(xm, h), head_of(xp, h)
        for first in (True, False) if up is not None else (False, True):
            if first:
                wait(r_p[i][k], buf.at[from_m, rows])
                if up is not None:
                    piece = buf.at[from_m, up]
                    send(r_rp[i][k], piece, piece, s, head_of(xp, zh))
            else:
                wait(r_m[i][k], buf.at[from_p, rows])
                if down is not None:
                    piece = buf.at[from_p, down]
                    send(r_rm[i][k], piece, piece, s, head_of(xm, zh))

    def far(i, h):
        buf, _, _, up, down = sets[i]
        k = 0 if h is zh else 1
        if up is not None:
            wait(r_rp[i][k], buf.at[head_of(x2, h), up])
        if down is not None:
            wait(r_rm[i][k], buf.at[head_of(x2, h), down])

    def onward(i):
        buf, _, rows, _, _ = sets[i]
        other = buf.at[head_of(x, oh), rows]
        wait(r_cross[i][0], other)
        send(r_p[i][1], other, other, s, head_of(xp, zh))
        send(r_m[i][1], other, other, s, head_of(xm, zh))

    def project(gg, first=False):
        rows = xn[gg]
        for i in range(3):
            part = jnp.dot(
                rows, qw[i, pl.ds(pl.multiple_of(gg * KC, KC), KC), :], preferred_element_type=F32
            )
            acc[i] = part if first else acc[i] + part

    def gproject(gg, first=False):
        rows = gn[gg]
        for i in range(3):
            block = gq[i, gg // 2, pl.ds((gg % 2) * 2, 2)].reshape(GKC, HD)
            part = jnp.dot(rows, block, preferred_element_type=F32)
            gacc[i] = part if first else gacc[i] + part

    relay(0, zh)
    onward(0)
    relay(1, zh)
    relay(2, zh)
    local[2].wait()
    for d in (1, 2, 3):
        wait(r_gqz[d - 1], gq.at[:, y, (zl + 4 - d) % 4, c])
    r_gqy, r_gqc = [role() for _ in range(3)], role()
    mine = gq.at[:, y, :, c]
    for d in (1, 3, 2):
        send(r_gqy[d - 1], mine, mine, seq_of((y + d) % 4, zl, c), g)
    onward(1)
    for i in (0, 1, 3):
        local[i].wait()
    project(g, True)
    project(head_of(xm, zh))
    onward(2)
    project(head_of(xp, zh))
    relay(0, oh)
    for d in (1, 2, 3):
        wait(r_gqy[d - 1], gq.at[:, (y + 4 - d) % 4, :, c])
    send(r_gqc, gq.at[:, :, :, c], gq.at[:, :, :, c], seq_of(y, zl, oc), g)
    project(head_of(x, oh))
    for i in range(3):
        far(i, zh)
    relay(1, oh)
    project(head_of(x2, zh))
    relay(2, oh)
    project(head_of(xm, oh))
    project(head_of(xp, oh))
    wait(r_gqc, gq.at[:, :, :, oc])
    gproject(g, True)
    for gg in (head_of(xm, zh), head_of(xp, zh), head_of(x2, zh), head_of(x, oh)):
        gproject(gg)
    gproject(head_of(xm, oh))
    gproject(head_of(xp, oh))
    far(0, oh)
    gproject(head_of(x2, oh))
    far(1, oh)
    far(2, oh)
    project(head_of(x2, oh))
    for i in range(3):
        for j in range(3):
            packed[i, j] = acc[i, :, j * HD : (j + 1) * HD].astype(BF16)
        packed[i, 3] = gacc[i].astype(BF16)

    own = [
        pltpu.make_async_copy(packed.at[0, zl], qb.at[zl], local_sem.at[6]),
        pltpu.make_async_copy(packed.at[1:3, zl], kv.at[:, y, c, zl], local_sem.at[7]),
    ]
    for one in own:
        one.start()
    r_q, r_kv = [role() for _ in range(3)], [role() for _ in range(3)]
    for d in (1, 2, 3):
        j = (zl + d) % 4
        there = seq_of(y, j, c)
        send(r_kv[d - 1], packed.at[1:3, j], kv.at[:, y, c, zl], there, g)
    for d in (1, 2, 3):
        j = (zl + d) % 4
        send(r_q[d - 1], packed.at[0, j], qb.at[zl], seq_of(y, j, c), g)
    for r, (_, _, here) in zip(r_perm, moved):
        wait(r, here)
    r_wz, r_gwz = [role() for _ in range(3)], [role() for _ in range(3)]
    for d in (1, 2, 3):
        there = seq_of(y, (zl + d) % 4, c)
        send(r_wz[d - 1], wt.at[y, zl, c], wt.at[y, zl, c], there, g)
        send(r_gwz[d - 1], gwt.at[y, zl, c], gwt.at[y, zl, c], there, g)
    zn = zl + 1 - 2 * (zl % 2)
    r_fz, r_gfz = role(), role()
    send(r_fz, fw.at[zl % 2, c], fw.at[zl % 2, c], seq_of(y, zn, c), g)
    send(r_gfz, gfw.at[zl % 2, c], gfw.at[zl % 2, c], seq_of(y, zn, c), g)
    r_kp, r_km = [role() for _ in range(4)], [role() for _ in range(4)]
    r_kc, r_kr = [role() for _ in range(4)], [role() for _ in range(4)]
    r_kcm, r_kcp, r_kc2 = role(), role(), role()
    for d in range(4):
        k = (zl + 4 - d) % 4
        block = kv.at[:, y, c, k]
        if d == 0:
            own[1].wait()
        else:
            wait(r_kv[d - 1], block)
        send(r_kp[d], block, block, seq_of(yp, zl, c), g)
        send(r_km[d], block, block, seq_of(ym, zl, c), g)
        send(r_kc[d], block, block, seq_of(y, zl, oc), g)
    own[0].wait()
    for d in (1, 2, 3):
        wait(r_q[d - 1], qb.at[(zl + 4 - d) % 4])

    def absorb(yy, cc, first=False):
        keys = kv[0, yy, cc].reshape(4 * ROWS, HD)
        values = kv[1, yy, cc].reshape(4 * ROWS, HD)
        queries = qb[...].reshape(4 * ROWS, HD)
        scores = lax.dot_general(keys, queries, NT, preferred_element_type=F32)
        highest = jnp.max(scores, axis=0, keepdims=True)
        if not first:
            before = top[...]
            highest = jnp.maximum(highest, before)
        expd = jnp.exp2((scores - highest) * SCALE2)
        total = jnp.sum(expd, axis=0, keepdims=True)
        mixed = lax.dot_general(values, expd.astype(BF16), TN, preferred_element_type=F32)
        top[...] = highest
        if first:
            tot[...] = total
            ot[...] = mixed
        else:
            shrink = jnp.exp2((before - highest) * SCALE2)
            tot[...] = tot[...] * shrink + total
            ot[...] = ot[...] * shrink + mixed

    absorb(y, c, True)
    for d in (0, 1):
        k = (zl + 4 - d) % 4
        wait(r_kp[d], kv.at[:, ym, c, k])
        send(r_kr[d], kv.at[:, ym, c, k], kv.at[:, ym, c, k], seq_of(yp, zl, c), g)
    for d in (2, 3):
        k = (zl + 4 - d) % 4
        wait(r_km[d], kv.at[:, yp, c, k])
        send(r_kr[d], kv.at[:, yp, c, k], kv.at[:, yp, c, k], seq_of(ym, zl, c), g)
    for d in (2, 3):
        wait(r_kp[d], kv.at[:, ym, c, (zl + 4 - d) % 4])
    send(r_kcm, kv.at[:, ym, c], kv.at[:, ym, c], seq_of(y, zl, oc), g)
    for d in (0, 1):
        wait(r_km[d], kv.at[:, yp, c, (zl + 4 - d) % 4])
    send(r_kcp, kv.at[:, yp, c], kv.at[:, yp, c], seq_of(y, zl, oc), g)
    for d in (1, 2, 3):
        wait(r_wz[d - 1], wt.at[y, (zl + 4 - d) % 4, c])
        wait(r_gwz[d - 1], gwt.at[y, (zl + 4 - d) % 4, c])
    r_w = [[role() for _ in range(6)] for _ in range(2)]
    for r, buf in zip(r_w, (wt, gwt)):
        block = buf.at[y, :, c]
        send(r[0], block, block, seq_of(yp, zl, c), g)
        send(r[1], block, block, seq_of(ym, zl, c), g)
    for d in range(4):
        wait(r_kc[d], kv.at[:, y, oc, (zl + 4 - d) % 4])
    absorb(y, oc)
    absorb(ym, c)
    absorb(yp, c)
    for d in range(4):
        wait(r_kr[d], kv.at[:, y2, c, (zl + 4 - d) % 4])
    send(r_kc2, kv.at[:, y2, c], kv.at[:, y2, c], seq_of(y, zl, oc), g)
    wait(r_kcm, kv.at[:, ym, oc])
    absorb(ym, oc)
    wait(r_kcp, kv.at[:, yp, oc])
    absorb(yp, oc)
    absorb(y2, c)
    wait(r_fz, fw.at[1 - zl % 2, c])
    wait(r_gfz, gfw.at[1 - zl % 2, c])
    r_fc, r_gfc = role(), role()
    send(r_fc, fw.at[:, c], fw.at[:, c], seq_of(y, zl, oc), g)
    send(r_gfc, gfw.at[:, c], gfw.at[:, c], seq_of(y, zl, oc), g)
    wait(r_kc2, kv.at[:, y2, oc])
    absorb(y2, oc)
    ob[...] = (ot[...] / tot[...]).T.astype(BF16)

    r_o = [[role(), role()] for _ in range(4)]
    for d in (0, 1, 2, 3):
        k = (zl + d) % 4
        block = ob.at[pl.ds(pl.multiple_of(k * ROWS, ROWS), ROWS), :]
        for e, h in enumerate((zh, oh)):
            if d == 0 and e == 0:
                pltpu.make_async_copy(block, at.at[x, zh, zl], recv_sem.at[r_o[0][0]]).start()
            else:
                send(r_o[d][e], block, at.at[x, zh, zl], seq_of(y, k, c), head_of(x, h))
    first_o = r_o[0][0]

    def arrived(j):
        d = (zl + 4 - j) % 4
        for e, h in enumerate((zh, oh)):
            wait(first_o + d * 2 + e, at.at[x, h, j])

    r_gx = [role() for _ in range(4)]
    r_mx = [role() for _ in range(4)]
    arrived(3)
    send(r_gx[0], at.at[x, :, 3], at.at[x, :, 3], s, head_of(xp, zh))
    send(r_gx[1], at.at[x, :, 3], at.at[x, :, 3], s, head_of(xm, zh))
    for j in range(3):
        arrived(j)
    send(r_mx[0], at.at[x, :, 0:3], at.at[x, :, 0:3], s, head_of(xp, zh))
    send(r_mx[1], at.at[x, :, 0:3], at.at[x, :, 0:3], s, head_of(xm, zh))

    for r, buf in zip(r_w, (wt, gwt)):
        a, b = buf.at[ym, 0:2, c], buf.at[yp, 2:4, c]
        wait(r[0], buf.at[ym, :, c])
        send(r[2], a, a, seq_of(yp, zl, c), g)
        wait(r[1], buf.at[yp, :, c])
        send(r[3], b, b, seq_of(ym, zl, c), g)
    wait(r_gx[0], at.at[xm, :, 3])
    send(r_gx[2], at.at[xm, 0, 3], at.at[xm, 0, 3], s, head_of(xp, zh))
    wait(r_gx[1], at.at[xp, :, 3])
    send(r_gx[3], at.at[xp, 1, 3], at.at[xp, 1, 3], s, head_of(xm, zh))
    wait(r_mx[0], at.at[xm, :, 0:3])
    send(r_mx[2], at.at[xm, 0, 0:3], at.at[xm, 0, 0:3], s, head_of(xp, zh))
    wait(r_mx[1], at.at[xp, :, 0:3])
    send(r_mx[3], at.at[xp, 1, 0:3], at.at[xp, 1, 0:3], s, head_of(xm, zh))
    for r, buf in zip(r_w, (wt, gwt)):
        wait(r[2], buf.at[y2, 0:2, c])
        wait(r[3], buf.at[y2, 2:4, c])
        send(r[4], buf.at[:, :, c], buf.at[:, :, c], seq_of(y, zl, oc), g)
    wait(r_fc, fw.at[:, oc])
    wait(r_gfc, gfw.at[:, oc])
    local[4].wait()
    local[5].wait()

    def gout_part(xx):
        total = None
        for h in range(2):
            block = gwt[xx, h * 2 : h * 2 + 2].reshape(GKC, HD)
            part = lax.dot_general(at[xx, h, 3], block, NT, preferred_element_type=F32)
            total = part if total is None else total + part
        return total

    def out_part(xx):
        total = None
        for h in range(2):
            rows = jnp.concatenate([at[xx, h, j] for j in range(3)], axis=1)
            block = wt[xx, h * 2 : h * 2 + 2].reshape(KC, 3 * HD)
            part = lax.dot_general(rows, block, NT, preferred_element_type=F32)
            total = part if total is None else total + part
        return total

    def column_sums(gains, weights, width, keep):
        n = width // 128
        row = jnp.concatenate([gains[pl.ds(g * n + i, 1), :] for i in range(n)], axis=1)
        rest = row - row.astype(BF16).astype(F32)
        at_row = lax.broadcasted_iota(jnp.int32, (16, width), 0)
        both = jnp.where(at_row == 0, row, jnp.where(at_row == 1, rest, 0.0)).astype(BF16)
        sums = jnp.dot(both, weights[...].reshape(width, 64), preferred_element_type=F32)
        sums = jnp.broadcast_to(jnp.sum(sums, axis=0, keepdims=True), (64, 64)).T
        for i in range(8):
            keep[i, 0:8, ROWS:] = sums[i * 8 : (i + 1) * 8]

    def spread(ref, width, gains, weights, keep, buf, roles):
        one = jnp.zeros((ROWS, 128), F32)
        two = jnp.zeros((ROWS, 128), F32)
        for i in range(width // 128):
            cols = ref[:, i * 128 : (i + 1) * 128]
            one = one + cols
            two = two + cols * cols
        center = jnp.sum(one, axis=1, keepdims=True) * (1.0 / width)
        parts = []
        for i in range(width // 128):
            row = gains[pl.ds(g * (width // 128) + i, 1), :]
            parts.append(((ref[:, i * 128 : (i + 1) * 128] - center) * row).astype(BF16))
        part = jnp.dot(
            jnp.concatenate(parts, axis=1), weights[...].reshape(width, 64),
            preferred_element_type=F32,
        ).T
        one = jnp.sum(one.T, axis=0, keepdims=True)
        two = jnp.sum(two.T, axis=0, keepdims=True)
        for i in range(8):
            keep[i, 0:8, 0:ROWS] = part[i * 8 : (i + 1) * 8]
            keep[i, 8:9, 0:ROWS] = one
            keep[i, 9:10, 0:ROWS] = two
        for d in range(1, 8):
            k = (g + d) % 8
            send(roles[d - 1], keep.at[k], buf.at[g], s, k)
        buf[g] = keep[g]

    def combine(width, buf, roles):
        for d in range(1, 8):
            wait(roles[d - 1], buf.at[(g + 8 - d) % 8])
        one, two = buf[0, 8:9, 0:ROWS], buf[0, 9:10, 0:ROWS]
        for i in range(1, 8):
            one, two = one + buf[i, 8:9, 0:ROWS], two + buf[i, 9:10, 0:ROWS]
        center, square = one * (0.125 / width), two * (0.125 / width)
        scale = lax.rsqrt(square - center * center + EPS)
        total = jnp.zeros((8, ROWS), F32)
        for i in range(8):
            shift = buf[i, 8:9, 0:ROWS] * (1.0 / width) - center
            total = total + (buf[i, 0:8, 0:ROWS] + shift * buf[i, 0:8, ROWS : ROWS + 1])
        return total * scale

    r_pg, r_pm, r_out = ([role() for _ in range(7)] for _ in range(3))
    column_sums(ggain, gfw, GKC, pg)
    column_sums(gain, fw, KC, pm)
    wait(r_w[1][4], gwt.at[:, :, oc])
    ghid[...] = gsb[...].astype(F32) + gout_part(x)
    ghid[...] += gout_part(xm)
    ghid[...] += gout_part(xp)
    wait(r_gx[2], at.at[x2, 0, 3])
    wait(r_gx[3], at.at[x2, 1, 3])
    ghid[...] += gout_part(x2)
    spread(ghid, GKC, ggain, gfw, pg, rg, r_pg)
    wait(r_w[0][4], wt.at[:, :, oc])
    hid[...] = sb[...].astype(F32) + out_part(x)
    hid[...] += out_part(xm)
    hid[...] += out_part(xp)
    gp[y, zl, c] = combine(GKC, rg, r_pg)
    near = [(d, e) for d in range(4) for e in range(2) if d or e]
    r_az, r_ay = [role() for _ in near], [role() for _ in range(3)]
    for r, (d, e) in zip(r_az, near):
        block = gp.at[y, zl, c]
        send(r, block, block, seq_of(y, (zl + d) % 4, oc if e else c), g)
    wait(r_mx[2], at.at[x2, 0, 0:3])
    wait(r_mx[3], at.at[x2, 1, 0:3])
    hid[...] += out_part(x2)
    spread(hid, KC, gain, fw, pm, rm, r_pm)
    for r, (d, e) in zip(r_az, near):
        wait(r, gp.at[y, (zl + 4 - d) % 4, oc if e else c])
    for d in (1, 2, 3):
        send(r_ay[d - 1], gp.at[y], gp.at[y], seq_of((y + d) % 4, zl, c), g)
    main_pred = combine(KC, rm, r_pm)
    for d in (1, 2, 3):
        wait(r_ay[d - 1], gp.at[(y + 4 - d) % 4])

    lane = lax.broadcasted_iota(jnp.int32, (8, 128), 1)
    pieces = []
    for yy in range(4):
        for zz in range(4):
            a0, a1 = gp[yy, zz, 0, :, 0:128], gp[yy, zz, 0, :, 128:192]
            b0, b1 = gp[yy, zz, 1, :, 0:64], gp[yy, zz, 1, :, 64:192]
            pieces += [a0, jnp.concatenate([a1, b0], axis=1), b1]
    slots = jnp.concatenate(pieces, axis=1)
    upper = slots.astype(BF16)
    lower = (slots - upper.astype(F32)).astype(BF16)
    both = jnp.concatenate([upper, lower], axis=0)
    picked = lax.dot_general(both, hot[...], NT, preferred_element_type=F32)
    picked = picked[0:8] + picked[8:16]

    first = s * ROWS
    frame = first // FRAME_TOK
    last = (first + ROWS - 1) // FRAME_TOK
    owned = first + lax.broadcasted_iota(jnp.int32, (8, ROWS), 1)
    strength = 1.0 + jnp.where(owned // FRAME_TOK == frame, flags[frame], flags[last]).astype(F32)
    outb[g] = picked + strength * (main_pred - picked)
    for d in range(1, 8):
        send(r_out[d - 1], outb.at[g], outb.at[g], s, (g + d) % 8)
    for d in range(1, 8):
        wait(r_out[d - 1], outb.at[(g + 8 - d) % 8])
    for i in range(8):
        out[i * 8 : (i + 1) * 8, :] = outb[i]

    for one in started:
        one.wait_send()

    @pl.when(jnp.logical_not(same))
    def _():
        for r, (src, there, _) in zip(r_perm, moved):
            copy(r, src, there, part_s, part_g).wait_send()


def per_device(
    stream, normed, qkv_weight, out_weight, final_gain, final_weight, guide_stream, guide_normed,
    guide_qkv, guide_out, guide_gain, guide_final, layout, flags,
):
    anyw = pl.BlockSpec(memory_space=pl.ANY)
    vmem = pl.BlockSpec(memory_space=pltpu.VMEM)
    smem = pl.BlockSpec(memory_space=pltpu.SMEM)
    v = pltpu.VMEM
    scratch = [
        v((8, ROWS, KC), BF16),
        v((8, ROWS, GKC), BF16),
        v((3, 5120, 384), BF16),
        v((3, 4, 4, 2, 64, HD), BF16),
        v((4, 4, 2, 160, 384), BF16),
        v((4, 4, 2, 64, HD), BF16),
        v((2, 2, 160, 64), BF16),
        v((2, 2, 64, 64), BF16),
        v((ROWS, KC), BF16),
        v((ROWS, GKC), BF16),
        v((3, ROWS, 384), F32),
        v((3, ROWS, HD), F32),
        v((3, 4, ROWS, HD), BF16),
        v((4, ROWS, HD), BF16),
        v((2, 4, 2, 4, ROWS, HD), BF16),
        v((1, 4 * ROWS), F32),
        v((1, 4 * ROWS), F32),
        v((HD, 4 * ROWS), F32),
        v((4 * ROWS, HD), BF16),
        v((4, 2, 4, ROWS, HD), BF16),
        v((ROWS, TOKENS), BF16),
        v((ROWS, KC), F32),
        v((ROWS, GKC), F32),
        v((160, 64), BF16),
        v((8, 16, 256), F32),
        v((8, 16, 256), F32),
        v((8, 16, 256), F32),
        v((8, 16, 256), F32),
        v((4, 4, 2, 8, ROWS), F32),
        v((8, 8, ROWS), F32),
        pltpu.SemaphoreType.DMA((192,)),
        pltpu.SemaphoreType.DMA((192,)),
        pltpu.SemaphoreType.DMA((8,)),
    ]
    guided = pl.pallas_call(
        body,
        out_shape=jax.ShapeDtypeStruct((64, ROWS), F32),
        in_specs=[anyw] * 4 + [vmem, vmem] + [anyw] * 4 + [vmem, anyw, vmem, smem],
        out_specs=vmem,
        scratch_shapes=scratch,
        compiler_params=pltpu.CompilerParams(
            collective_id=0, has_side_effects=True, vmem_limit_bytes=56 * 1024 * 1024
        ),
        cost_estimate=pl.CostEstimate(
            flops=6_000_000_000, bytes_accessed=20_000_000, transcendentals=5_000_000
        ),
    )(
        stream, normed, jnp.transpose(qkv_weight, (1, 0, 2)), out_weight.T,
        final_gain.reshape(40, 128), final_weight.T, guide_stream, guide_normed,
        jnp.transpose(guide_qkv, (1, 0, 2)), guide_out.T, guide_gain.reshape(16, 128), guide_final,
        layout.reshape(48, 128), flags,
    )
    return guided.T


def solution(mesh):
    placed = (
        P("seq", "head"),
        P("seq", "head"),
        P(None, None, "head"),
        P("head", "seq"),
        P(),
        P("seq", None),
        P("seq", "head"),
        P("seq", "head"),
        P("seq", None, "head"),
        P("head", "seq"),
        P(),
        P("seq", None),
        P(),
        P(),
    )
    return jax.shard_map(
        per_device, mesh=mesh, in_specs=placed, out_specs=P("seq", None), check_vma=False
    )
```

time: 147 us -> 133 us (0.905); the launches traced: 146 us -> 133 us
  Pallas kernels: 143 us -> 132 us
  local copies, waits for them, and re-layouts: 2.95 us -> 1.47 us
    pallas_call x1, Pallas kernels: 143 us -> 132 us  [per_device(): pl.pallas_call(body, out_shape=jax.ShapeDtypeStruct((64, ROWS), F32), in_...]
    unnamed x2 -> x1, local copies, waits for them, and re-layouts: 2.95 us -> 1.47 us
where the time goes in v2:
time: 133 us
  Pallas kernels  132 us (99%)
  local copies, waits for them, and re-layouts  1.47 us (1%)
    pallas_call x1, Pallas kernels, per_device(): pl.pallas_call(body, out_shape=jax.ShapeDtypeStruct((64, ROWS), F32), in_...  132 us

profile of v2, /device:TPU:1, one launch (start us, length us, event | category | flops | bytes accessed | tf_op | source)
XLA Modules:
  0.0 133.2 jit_solution(1800173612115873102)
XLA Ops:
  0.0 131.7 %shard_map.136 = f32[64,192]{1,0:T(8,128)} custom-call(bf16[192,640]{1,0:T(8,128)(2,1)} %stream.1, bf16[192,640]{1,0:T(8,128)(2,1)} %normed.1, bf16[3,5120,384]{2,1,0:T(8,128)(2,1)} %bitcast.10, bf16[160,384]{1,0:T(8,128)(2,1)} %bitcast.11, f32[40,128]{1,0:T(8,128)} %bitcast.15, bf16[64,160]{1,0:T(8,128)(2,1)} %bitcast.13, bf16[192,256]{1,0:T(8,128)(2,1)} %gstream.1, ...), custom_call_target="tpu_custom_call" | custom-call | flops 6000000000 | bytes 20000000 | tf_op jit(solution)/shard_map/pallas_call | solution.py:565
  131.7 1.5 %copy.16 = f32[192,64]{0,1:T(8,128)} copy(f32[192,64]{0,1:T(8,128)} %bitcast.9) | data formatting | bytes 98304

commit v3 on v2

--- a/solution.py
+++ b/solution.py
@@ -60,6 +60,11 @@
         one = copy(r, src, dst, ss, gg)
         one.start()
         started.append(one)
+
+    def flush(upto):
+        for one in started[:upto]:
+            one.wait_send()
+        del started[:upto]
 
     def wait(r, dst):
         copy(r, dst, dst, seq_of(y, zl, oc), g).wait_recv()
@@ -178,10 +183,6 @@
             part = jnp.dot(rows, block, preferred_element_type=F32)
             gacc[i] = part if first else gacc[i] + part
 
-    relay(0, zh)
-    onward(0)
-    relay(1, zh)
-    relay(2, zh)
     local[2].wait()
     for d in (1, 2, 3):
         wait(r_gqz[d - 1], gq.at[:, y, (zl + 4 - d) % 4, c])
@@ -189,17 +190,32 @@
     mine = gq.at[:, y, :, c]
     for d in (1, 3, 2):
         send(r_gqy[d - 1], mine, mine, seq_of((y + d) % 4, zl, c), g)
+    relay(0, zh)
+    onward(0)
+    relay(1, zh)
+    relay(2, zh)
     onward(1)
     for i in (0, 1, 3):
         local[i].wait()
     project(g, True)
     project(head_of(xm, zh))
     onward(2)
+    for d in (1, 2, 3):
+        wait(r_gqy[d - 1], gq.at[:, (y + 4 - d) % 4, :, c])
+    send(r_gqc, gq.at[:, :, :, c], gq.at[:, :, :, c], seq_of(y, zl, oc), g)
+    for r, (_, _, here) in zip(r_perm, moved):
+        wait(r, here)
+    r_wz, r_gwz = [role() for _ in range(3)], [role() for _ in range(3)]
+    for d in (1, 2, 3):
+        there = seq_of(y, (zl + d) % 4, c)
+        send(r_wz[d - 1], wt.at[y, zl, c], wt.at[y, zl, c], there, g)
+        send(r_gwz[d - 1], gwt.at[y, zl, c], gwt.at[y, zl, c], there, g)
+    zn = zl + 1 - 2 * (zl % 2)
+    r_fz, r_gfz = role(), role()
+    send(r_fz, fw.at[zl % 2, c], fw.at[zl % 2, c], seq_of(y, zn, c), g)
+    send(r_gfz, gfw.at[zl % 2, c], gfw.at[zl % 2, c], seq_of(y, zn, c), g)
     project(head_of(xp, zh))
     relay(0, oh)
-    for d in (1, 2, 3):
-        wait(r_gqy[d - 1], gq.at[:, (y + 4 - d) % 4, :, c])
-    send(r_gqc, gq.at[:, :, :, c], gq.at[:, :, :, c], seq_of(y, zl, oc), g)
     project(head_of(x, oh))
     for i in range(3):
         far(i, zh)
@@ -224,6 +240,8 @@
             packed[i, j] = acc[i, :, j * HD : (j + 1) * HD].astype(BF16)
         packed[i, 3] = gacc[i].astype(BF16)
 
+    sent_a = len(started)
+
     own = [
         pltpu.make_async_copy(packed.at[0, zl], qb.at[zl], local_sem.at[6]),
         pltpu.make_async_copy(packed.at[1:3, zl], kv.at[:, y, c, zl], local_sem.at[7]),
@@ -238,17 +256,6 @@
     for d in (1, 2, 3):
         j = (zl + d) % 4
         send(r_q[d - 1], packed.at[0, j], qb.at[zl], seq_of(y, j, c), g)
-    for r, (_, _, here) in zip(r_perm, moved):
-        wait(r, here)
-    r_wz, r_gwz = [role() for _ in range(3)], [role() for _ in range(3)]
-    for d in (1, 2, 3):
-        there = seq_of(y, (zl + d) % 4, c)
-        send(r_wz[d - 1], wt.at[y, zl, c], wt.at[y, zl, c], there, g)
-        send(r_gwz[d - 1], gwt.at[y, zl, c], gwt.at[y, zl, c], there, g)
-    zn = zl + 1 - 2 * (zl % 2)
-    r_fz, r_gfz = role(), role()
-    send(r_fz, fw.at[zl % 2, c], fw.at[zl % 2, c], seq_of(y, zn, c), g)
-    send(r_gfz, gfw.at[zl % 2, c], gfw.at[zl % 2, c], seq_of(y, zn, c), g)
     r_kp, r_km = [role() for _ in range(4)], [role() for _ in range(4)]
     r_kc, r_kr = [role() for _ in range(4)], [role() for _ in range(4)]
     r_kcm, r_kcp, r_kc2 = role(), role(), role()
@@ -328,6 +335,7 @@
     r_fc, r_gfc = role(), role()
     send(r_fc, fw.at[:, c], fw.at[:, c], seq_of(y, zl, oc), g)
     send(r_gfc, gfw.at[:, c], gfw.at[:, c], seq_of(y, zl, oc), g)
+    flush(sent_a)
     wait(r_kc2, kv.at[:, y2, oc])
     absorb(y2, oc)
     ob[...] = (ot[...] / tot[...]).T.astype(BF16)
@@ -451,6 +459,7 @@
         return total * scale
 
     r_pg, r_pm, r_out = ([role() for _ in range(7)] for _ in range(3))
+    sent_d = len(started)
     column_sums(ggain, gfw, GKC, pg)
     column_sums(gain, fw, KC, pm)
     wait(r_w[1][4], gwt.at[:, :, oc])
@@ -475,6 +484,13 @@
     wait(r_mx[3], at.at[x2, 1, 0:3])
     hid[...] += out_part(x2)
     spread(hid, KC, gain, fw, pm, rm, r_pm)
+    flush(sent_d)
+
+    @pl.when(jnp.logical_not(same))
+    def _():
+        for r, (src, there, _) in zip(r_perm, moved):
+            copy(r, src, there, part_s, part_g).wait_send()
+
     for r, (d, e) in zip(r_az, near):
         wait(r, gp.at[y, (zl + 4 - d) % 4, oc if e else c])
     for d in (1, 2, 3):
@@ -505,18 +521,13 @@
     outb[g] = picked + strength * (main_pred - picked)
     for d in range(1, 8):
         send(r_out[d - 1], outb.at[g], outb.at[g], s, (g + d) % 8)
+    flush(len(started) - 7)
     for d in range(1, 8):
         wait(r_out[d - 1], outb.at[(g + 8 - d) % 8])
     for i in range(8):
         out[i * 8 : (i + 1) * 8, :] = outb[i]
 
-    for one in started:
-        one.wait_send()
-
-    @pl.when(jnp.logical_not(same))
-    def _():
-        for r, (src, there, _) in zip(r_perm, moved):
-            copy(r, src, there, part_s, part_g).wait_send()
+    flush(len(started))
 
 
 def per_device(

time: 133 us -> 131 us (0.985)
  Pallas kernels: 132 us -> 130 us
    pallas_call x1, Pallas kernels: 132 us -> 130 us  [per_device(): pl.pallas_call(body, out_shape=jax.ShapeDtypeStruct((64, ROWS), F32), in_...]
where the time goes in v3:
time: 131 us
  Pallas kernels  130 us (99%)
  local copies, waits for them, and re-layouts  1.47 us (1%)
    pallas_call x1, Pallas kernels, per_device(): pl.pallas_call(body, out_shape=jax.ShapeDtypeStruct((64, ROWS), F32), in_...  130 us

profile of v3, /device:TPU:1, one launch (start us, length us, event | category | flops | bytes accessed | tf_op | source)
XLA Modules:
  0.0 131.3 jit_solution(7786648855825673696)
XLA Ops:
  0.0 129.8 %shard_map.136 = f32[64,192]{1,0:T(8,128)} custom-call(bf16[192,640]{1,0:T(8,128)(2,1)} %stream.1, bf16[192,640]{1,0:T(8,128)(2,1)} %normed.1, bf16[3,5120,384]{2,1,0:T(8,128)(2,1)} %bitcast.10, bf16[160,384]{1,0:T(8,128)(2,1)} %bitcast.11, f32[40,128]{1,0:T(8,128)} %bitcast.15, bf16[64,160]{1,0:T(8,128)(2,1)} %bitcast.13, bf16[192,256]{1,0:T(8,128)(2,1)} %gstream.1, ...), custom_call_target="tpu_custom_call" | custom-call | flops 6000000000 | bytes 20000000 | tf_op jit(solution)/shard_map/pallas_call | solution.py:576
  129.8 1.5 %copy.16 = f32[192,64]{0,1:T(8,128)} copy(f32[192,64]{0,1:T(8,128)} %bitcast.9) | data formatting | bytes 98304

commit v4 on v3

--- a/solution.py
+++ b/solution.py
@@ -61,6 +61,45 @@
         one.start()
         started.append(one)
 
+    maybe = []
+
+    def line(block, own):
+        up, down = [role() for _ in range(3)], [role() for _ in range(3)]
+
+        def give(when, r, src, dst, zz):
+            @pl.when(when)
+            def _():
+                copy(r, src, dst, seq_of(y, zz, c), g).start()
+
+            maybe.append((when, r, dst, zz))
+
+        def step(k):
+            if k == 0:
+                give(zl < 3, up[0], own, block(zl), zl + 1)
+                give(zl > 0, down[0], own, block(zl), zl - 1)
+                return
+
+            @pl.when(zl >= k)
+            def _():
+                wait(up[k - 1], block(zl - k))
+
+            @pl.when(zl <= 3 - k)
+            def _():
+                wait(down[k - 1], block(zl + k))
+
+            if k < 3:
+                a, b = jnp.maximum(zl - k, 0), jnp.minimum(zl + k, 3)
+                give(jnp.logical_and(zl >= k, zl < 3), up[k], block(a), block(a), zl + 1)
+                give(jnp.logical_and(zl <= 3 - k, zl > 0), down[k], block(b), block(b), zl - 1)
+
+        return step
+
+    def flush_lines():
+        for when, r, dst, zz in maybe:
+            @pl.when(when)
+            def _():
+                copy(r, dst, dst, seq_of(y, zz, c), g).wait_send()
+
     def flush(upto):
         for one in started[:upto]:
             one.wait_send()
@@ -102,9 +141,8 @@
 
     pl.semaphore_wait(barrier, len(peers) + 1 - same.astype(jnp.int32))
 
-    r_gqz = [role() for _ in range(3)]
-    for d in (1, 2, 3):
-        send(r_gqz[d - 1], gqkv_t, gq.at[:, y, zl, c], seq_of(y, (zl + d) % 4, c), g)
+    gq_line = line(lambda zz: gq.at[:, y, zz, c], gqkv_t)
+    gq_line(0)
     low, high = pl.ds(0, HALF), pl.ds(HALF, HALF)
     whole = pl.ds(0, ROWS)
     sets = [
@@ -183,17 +221,18 @@
             part = jnp.dot(rows, block, preferred_element_type=F32)
             gacc[i] = part if first else gacc[i] + part
 
+    gq_line(1)
+    relay(0, zh)
+    onward(0)
+    gq_line(2)
+    relay(1, zh)
+    relay(2, zh)
+    gq_line(3)
     local[2].wait()
-    for d in (1, 2, 3):
-        wait(r_gqz[d - 1], gq.at[:, y, (zl + 4 - d) % 4, c])
     r_gqy, r_gqc = [role() for _ in range(3)], role()
     mine = gq.at[:, y, :, c]
     for d in (1, 3, 2):
         send(r_gqy[d - 1], mine, mine, seq_of((y + d) % 4, zl, c), g)
-    relay(0, zh)
-    onward(0)
-    relay(1, zh)
-    relay(2, zh)
     onward(1)
     for i in (0, 1, 3):
         local[i].wait()
@@ -205,11 +244,9 @@
     send(r_gqc, gq.at[:, :, :, c], gq.at[:, :, :, c], seq_of(y, zl, oc), g)
     for r, (_, _, here) in zip(r_perm, moved):
         wait(r, here)
-    r_wz, r_gwz = [role() for _ in range(3)], [role() for _ in range(3)]
-    for d in (1, 2, 3):
-        there = seq_of(y, (zl + d) % 4, c)
-        send(r_wz[d - 1], wt.at[y, zl, c], wt.at[y, zl, c], there, g)
-        send(r_gwz[d - 1], gwt.at[y, zl, c], gwt.at[y, zl, c], there, g)
+    w_lines = [line(lambda zz, buf=buf: buf.at[y, zz, c], buf.at[y, zl, c]) for buf in (wt, gwt)]
+    for one in w_lines:
+        one(0)
     zn = zl + 1 - 2 * (zl % 2)
     r_fz, r_gfz = role(), role()
     send(r_fz, fw.at[zl % 2, c], fw.at[zl % 2, c], seq_of(y, zn, c), g)
@@ -222,6 +259,8 @@
     relay(1, oh)
     project(head_of(x2, zh))
     relay(2, oh)
+    for one in w_lines:
+        one(1)
     project(head_of(xm, oh))
     project(head_of(xp, oh))
     wait(r_gqc, gq.at[:, :, :, oc])
@@ -256,6 +295,8 @@
     for d in (1, 2, 3):
         j = (zl + d) % 4
         send(r_q[d - 1], packed.at[0, j], qb.at[zl], seq_of(y, j, c), g)
+    for one in w_lines:
+        one(2)
     r_kp, r_km = [role() for _ in range(4)], [role() for _ in range(4)]
     r_kc, r_kr = [role() for _ in range(4)], [role() for _ in range(4)]
     r_kcm, r_kcp, r_kc2 = role(), role(), role()
@@ -268,6 +309,7 @@
             wait(r_kv[d - 1], block)
         send(r_kp[d], block, block, seq_of(yp, zl, c), g)
         send(r_km[d], block, block, seq_of(ym, zl, c), g)
+        send(r_kr[d], block, block, seq_of(y2, zl, c), g)
         send(r_kc[d], block, block, seq_of(y, zl, oc), g)
     own[0].wait()
     for d in (1, 2, 3):
@@ -295,31 +337,22 @@
             ot[...] = ot[...] * shrink + mixed
 
     absorb(y, c, True)
-    for d in (0, 1):
-        k = (zl + 4 - d) % 4
-        wait(r_kp[d], kv.at[:, ym, c, k])
-        send(r_kr[d], kv.at[:, ym, c, k], kv.at[:, ym, c, k], seq_of(yp, zl, c), g)
-    for d in (2, 3):
-        k = (zl + 4 - d) % 4
-        wait(r_km[d], kv.at[:, yp, c, k])
-        send(r_kr[d], kv.at[:, yp, c, k], kv.at[:, yp, c, k], seq_of(ym, zl, c), g)
-    for d in (2, 3):
+    for d in range(4):
+        wait(r_kc[d], kv.at[:, y, oc, (zl + 4 - d) % 4])
+    absorb(y, oc)
+    for d in range(4):
         wait(r_kp[d], kv.at[:, ym, c, (zl + 4 - d) % 4])
     send(r_kcm, kv.at[:, ym, c], kv.at[:, ym, c], seq_of(y, zl, oc), g)
-    for d in (0, 1):
+    for d in range(4):
         wait(r_km[d], kv.at[:, yp, c, (zl + 4 - d) % 4])
     send(r_kcp, kv.at[:, yp, c], kv.at[:, yp, c], seq_of(y, zl, oc), g)
-    for d in (1, 2, 3):
-        wait(r_wz[d - 1], wt.at[y, (zl + 4 - d) % 4, c])
-        wait(r_gwz[d - 1], gwt.at[y, (zl + 4 - d) % 4, c])
+    for one in w_lines:
+        one(3)
     r_w = [[role() for _ in range(6)] for _ in range(2)]
     for r, buf in zip(r_w, (wt, gwt)):
         block = buf.at[y, :, c]
         send(r[0], block, block, seq_of(yp, zl, c), g)
         send(r[1], block, block, seq_of(ym, zl, c), g)
-    for d in range(4):
-        wait(r_kc[d], kv.at[:, y, oc, (zl + 4 - d) % 4])
-    absorb(y, oc)
     absorb(ym, c)
     absorb(yp, c)
     for d in range(4):
@@ -351,6 +384,22 @@
                 send(r_o[d][e], block, at.at[x, zh, zl], seq_of(y, k, c), head_of(x, h))
     first_o = r_o[0][0]
 
+    def column_sums(gains, weights, width, keep):
+        n = width // 128
+        row = jnp.concatenate([gains[pl.ds(g * n + i, 1), :] for i in range(n)], axis=1)
+        rest = row - row.astype(BF16).astype(F32)
+        at_row = lax.broadcasted_iota(jnp.int32, (16, width), 0)
+        both = jnp.where(at_row == 0, row, jnp.where(at_row == 1, rest, 0.0)).astype(BF16)
+        sums = jnp.dot(both, weights[...].reshape(width, 64), preferred_element_type=F32)
+        sums = jnp.broadcast_to(jnp.sum(sums, axis=0, keepdims=True), (64, 64)).T
+        for i in range(8):
+            keep[i, 0:8, ROWS:] = sums[i * 8 : (i + 1) * 8]
+
+    wait(r_fc, fw.at[:, oc])
+    wait(r_gfc, gfw.at[:, oc])
+    column_sums(ggain, gfw, GKC, pg)
+    column_sums(gain, fw, KC, pm)
+
     def arrived(j):
         d = (zl + 4 - j) % 4
         for e, h in enumerate((zh, oh)):
@@ -384,8 +433,6 @@
         wait(r[2], buf.at[y2, 0:2, c])
         wait(r[3], buf.at[y2, 2:4, c])
         send(r[4], buf.at[:, :, c], buf.at[:, :, c], seq_of(y, zl, oc), g)
-    wait(r_fc, fw.at[:, oc])
-    wait(r_gfc, gfw.at[:, oc])
     local[4].wait()
     local[5].wait()
 
@@ -405,17 +452,6 @@
             part = lax.dot_general(rows, block, NT, preferred_element_type=F32)
             total = part if total is None else total + part
         return total
-
-    def column_sums(gains, weights, width, keep):
-        n = width // 128
-        row = jnp.concatenate([gains[pl.ds(g * n + i, 1), :] for i in range(n)], axis=1)
-        rest = row - row.astype(BF16).astype(F32)
-        at_row = lax.broadcasted_iota(jnp.int32, (16, width), 0)
-        both = jnp.where(at_row == 0, row, jnp.where(at_row == 1, rest, 0.0)).astype(BF16)
-        sums = jnp.dot(both, weights[...].reshape(width, 64), preferred_element_type=F32)
-        sums = jnp.broadcast_to(jnp.sum(sums, axis=0, keepdims=True), (64, 64)).T
-        for i in range(8):
-            keep[i, 0:8, ROWS:] = sums[i * 8 : (i + 1) * 8]
 
     def spread(ref, width, gains, weights, keep, buf, roles):
         one = jnp.zeros((ROWS, 128), F32)
@@ -460,8 +496,6 @@
 
     r_pg, r_pm, r_out = ([role() for _ in range(7)] for _ in range(3))
     sent_d = len(started)
-    column_sums(ggain, gfw, GKC, pg)
-    column_sums(gain, fw, KC, pm)
     wait(r_w[1][4], gwt.at[:, :, oc])
     ghid[...] = gsb[...].astype(F32) + gout_part(x)
     ghid[...] += gout_part(xm)
@@ -474,17 +508,18 @@
     hid[...] = sb[...].astype(F32) + out_part(x)
     hid[...] += out_part(xm)
     hid[...] += out_part(xp)
+    wait(r_mx[2], at.at[x2, 0, 0:3])
+    wait(r_mx[3], at.at[x2, 1, 0:3])
+    hid[...] += out_part(x2)
+    spread(hid, KC, gain, fw, pm, rm, r_pm)
     gp[y, zl, c] = combine(GKC, rg, r_pg)
     near = [(d, e) for d in range(4) for e in range(2) if d or e]
     r_az, r_ay = [role() for _ in near], [role() for _ in range(3)]
     for r, (d, e) in zip(r_az, near):
         block = gp.at[y, zl, c]
         send(r, block, block, seq_of(y, (zl + d) % 4, oc if e else c), g)
-    wait(r_mx[2], at.at[x2, 0, 0:3])
-    wait(r_mx[3], at.at[x2, 1, 0:3])
-    hid[...] += out_part(x2)
-    spread(hid, KC, gain, fw, pm, rm, r_pm)
     flush(sent_d)
+    flush_lines()
 
     @pl.when(jnp.logical_not(same))
     def _():

time: 131 us -> 137 us (1.046)
  Pallas kernels: 130 us -> 136 us
    pallas_call x1, Pallas kernels: 130 us -> 136 us  [per_device(): pl.pallas_call(body, out_shape=jax.ShapeDtypeStruct((64, ROWS), F32), in_...]
where the time goes in v4:
time: 137 us
  Pallas kernels  136 us (99%)
  local copies, waits for them, and re-layouts  1.47 us (1%)
    pallas_call x1, Pallas kernels, per_device(): pl.pallas_call(body, out_shape=jax.ShapeDtypeStruct((64, ROWS), F32), in_...  136 us

profile of v4, /device:TPU:1, one launch (start us, length us, event | category | flops | bytes accessed | tf_op | source)
XLA Modules:
  0.0 137.0 jit_solution(17866387608533295471)
XLA Ops:
  0.0 135.5 %shard_map.136 = f32[64,192]{1,0:T(8,128)} custom-call(bf16[192,640]{1,0:T(8,128)(2,1)} %stream.1, bf16[192,640]{1,0:T(8,128)(2,1)} %normed.1, bf16[3,5120,384]{2,1,0:T(8,128)(2,1)} %bitcast.10, bf16[160,384]{1,0:T(8,128)(2,1)} %bitcast.11, f32[40,128]{1,0:T(8,128)} %bitcast.15, bf16[64,160]{1,0:T(8,128)(2,1)} %bitcast.13, bf16[192,256]{1,0:T(8,128)(2,1)} %gstream.1, ...), custom_call_target="tpu_custom_call" | custom-call | flops 6000000000 | bytes 20000000 | tf_op jit(solution)/shard_map/pallas_call | solution.py:611
  135.6 1.5 %copy.16 = f32[192,64]{0,1:T(8,128)} copy(f32[192,64]{0,1:T(8,128)} %bitcast.9) | data formatting | bytes 98304

commit v5 on v2

--- a/solution.py
+++ b/solution.py
@@ -61,6 +61,11 @@
         one.start()
         started.append(one)
 
+    def flush(upto):
+        for one in started[:upto]:
+            one.wait_send()
+        del started[:upto]
+
     def wait(r, dst):
         copy(r, dst, dst, seq_of(y, zl, oc), g).wait_recv()
 
@@ -97,9 +102,6 @@
 
     pl.semaphore_wait(barrier, len(peers) + 1 - same.astype(jnp.int32))
 
-    r_gqz = [role() for _ in range(3)]
-    for d in (1, 2, 3):
-        send(r_gqz[d - 1], gqkv_t, gq.at[:, y, zl, c], seq_of(y, (zl + d) % 4, c), g)
     low, high = pl.ds(0, HALF), pl.ds(HALF, HALF)
     whole = pl.ds(0, ROWS)
     sets = [
@@ -182,32 +184,63 @@
     onward(0)
     relay(1, zh)
     relay(2, zh)
-    local[2].wait()
-    for d in (1, 2, 3):
-        wait(r_gqz[d - 1], gq.at[:, y, (zl + 4 - d) % 4, c])
-    r_gqy, r_gqc = [role() for _ in range(3)], role()
-    mine = gq.at[:, y, :, c]
-    for d in (1, 3, 2):
-        send(r_gqy[d - 1], mine, mine, seq_of((y + d) % 4, zl, c), g)
     onward(1)
     for i in (0, 1, 3):
         local[i].wait()
     project(g, True)
     project(head_of(xm, zh))
     onward(2)
+    r_gqz = [role() for _ in range(3)]
+    for d in (1, 2, 3):
+        send(r_gqz[d - 1], gqkv_t, gq.at[:, y, zl, c], seq_of(y, (zl + d) % 4, c), g)
     project(head_of(xp, zh))
     relay(0, oh)
-    for d in (1, 2, 3):
-        wait(r_gqy[d - 1], gq.at[:, (y + 4 - d) % 4, :, c])
-    send(r_gqc, gq.at[:, :, :, c], gq.at[:, :, :, c], seq_of(y, zl, oc), g)
     project(head_of(x, oh))
     for i in range(3):
         far(i, zh)
     relay(1, oh)
     project(head_of(x2, zh))
     relay(2, oh)
+    local[2].wait()
+    for d in (1, 2, 3):
+        wait(r_gqz[d - 1], gq.at[:, y, (zl + 4 - d) % 4, c])
+    r_gqy, r_gqc = [role() for _ in range(3)], role()
+    mine = gq.at[:, y, :, c]
+    for d in (1, 3, 2):
+        send(r_gqy[d - 1], mine, mine, seq_of((y + d) % 4, zl, c), g)
     project(head_of(xm, oh))
     project(head_of(xp, oh))
+    far(1, oh)
+    far(2, oh)
+    project(head_of(x2, oh))
+    for i in range(3):
+        for j in range(3):
+            packed[i, j] = acc[i, :, j * HD : (j + 1) * HD].astype(BF16)
+    sent_a = len(started)
+
+    r_q, r_kv = [role() for _ in range(3)], [role() for _ in range(3)]
+
+    def heads(guide):
+        for d in (1, 2, 3):
+            j = (zl + d) % 4
+            there = seq_of(y, j, c)
+            both = [
+                copy(r_kv[d - 1], packed.at[1:3, j], kv.at[:, y, c, zl], there, g),
+                copy(r_q[d - 1], packed.at[0, j], qb.at[zl], there, g),
+            ]
+
+            @pl.when(j == 3 if guide else j != 3)
+            def _():
+                for one in both:
+                    one.start()
+
+            if guide:
+                started.extend(both)
+
+    heads(False)
+    for d in (1, 2, 3):
+        wait(r_gqy[d - 1], gq.at[:, (y + 4 - d) % 4, :, c])
+    send(r_gqc, gq.at[:, :, :, c], gq.at[:, :, :, c], seq_of(y, zl, oc), g)
     wait(r_gqc, gq.at[:, :, :, oc])
     gproject(g, True)
     for gg in (head_of(xm, zh), head_of(xp, zh), head_of(x2, zh), head_of(x, oh)):
@@ -216,28 +249,15 @@
     gproject(head_of(xp, oh))
     far(0, oh)
     gproject(head_of(x2, oh))
-    far(1, oh)
-    far(2, oh)
-    project(head_of(x2, oh))
     for i in range(3):
-        for j in range(3):
-            packed[i, j] = acc[i, :, j * HD : (j + 1) * HD].astype(BF16)
         packed[i, 3] = gacc[i].astype(BF16)
-
+    heads(True)
     own = [
         pltpu.make_async_copy(packed.at[0, zl], qb.at[zl], local_sem.at[6]),
         pltpu.make_async_copy(packed.at[1:3, zl], kv.at[:, y, c, zl], local_sem.at[7]),
     ]
     for one in own:
         one.start()
-    r_q, r_kv = [role() for _ in range(3)], [role() for _ in range(3)]
-    for d in (1, 2, 3):
-        j = (zl + d) % 4
-        there = seq_of(y, j, c)
-        send(r_kv[d - 1], packed.at[1:3, j], kv.at[:, y, c, zl], there, g)
-    for d in (1, 2, 3):
-        j = (zl + d) % 4
-        send(r_q[d - 1], packed.at[0, j], qb.at[zl], seq_of(y, j, c), g)
     for r, (_, _, here) in zip(r_perm, moved):
         wait(r, here)
     r_wz, r_gwz = [role() for _ in range(3)], [role() for _ in range(3)]
@@ -302,14 +322,6 @@
     for d in (0, 1):
         wait(r_km[d], kv.at[:, yp, c, (zl + 4 - d) % 4])
     send(r_kcp, kv.at[:, yp, c], kv.at[:, yp, c], seq_of(y, zl, oc), g)
-    for d in (1, 2, 3):
-        wait(r_wz[d - 1], wt.at[y, (zl + 4 - d) % 4, c])
-        wait(r_gwz[d - 1], gwt.at[y, (zl + 4 - d) % 4, c])
-    r_w = [[role() for _ in range(6)] for _ in range(2)]
-    for r, buf in zip(r_w, (wt, gwt)):
-        block = buf.at[y, :, c]
-        send(r[0], block, block, seq_of(yp, zl, c), g)
-        send(r[1], block, block, seq_of(ym, zl, c), g)
     for d in range(4):
         wait(r_kc[d], kv.at[:, y, oc, (zl + 4 - d) % 4])
     absorb(y, oc)
@@ -318,6 +330,14 @@
     for d in range(4):
         wait(r_kr[d], kv.at[:, y2, c, (zl + 4 - d) % 4])
     send(r_kc2, kv.at[:, y2, c], kv.at[:, y2, c], seq_of(y, zl, oc), g)
+    for d in (1, 2, 3):
+        wait(r_wz[d - 1], wt.at[y, (zl + 4 - d) % 4, c])
+        wait(r_gwz[d - 1], gwt.at[y, (zl + 4 - d) % 4, c])
+    r_w = [[role() for _ in range(6)] for _ in range(2)]
+    for r, buf in ((r_w[1], gwt), (r_w[0], wt)):
+        block = buf.at[y, :, c]
+        send(r[0], block, block, seq_of(yp, zl, c), g)
+        send(r[1], block, block, seq_of(ym, zl, c), g)
     wait(r_kcm, kv.at[:, ym, oc])
     absorb(ym, oc)
     wait(r_kcp, kv.at[:, yp, oc])
@@ -328,6 +348,7 @@
     r_fc, r_gfc = role(), role()
     send(r_fc, fw.at[:, c], fw.at[:, c], seq_of(y, zl, oc), g)
     send(r_gfc, gfw.at[:, c], gfw.at[:, c], seq_of(y, zl, oc), g)
+    flush(sent_a)
     wait(r_kc2, kv.at[:, y2, oc])
     absorb(y2, oc)
     ob[...] = (ot[...] / tot[...]).T.astype(BF16)
@@ -343,6 +364,22 @@
                 send(r_o[d][e], block, at.at[x, zh, zl], seq_of(y, k, c), head_of(x, h))
     first_o = r_o[0][0]
 
+    def column_sums(gains, weights, width, keep):
+        n = width // 128
+        row = jnp.concatenate([gains[pl.ds(g * n + i, 1), :] for i in range(n)], axis=1)
+        rest = row - row.astype(BF16).astype(F32)
+        at_row = lax.broadcasted_iota(jnp.int32, (16, width), 0)
+        both = jnp.where(at_row == 0, row, jnp.where(at_row == 1, rest, 0.0)).astype(BF16)
+        sums = jnp.dot(both, weights[...].reshape(width, 64), preferred_element_type=F32)
+        sums = jnp.broadcast_to(jnp.sum(sums, axis=0, keepdims=True), (64, 64)).T
+        for i in range(8):
+            keep[i, 0:8, ROWS:] = sums[i * 8 : (i + 1) * 8]
+
+    wait(r_fc, fw.at[:, oc])
+    wait(r_gfc, gfw.at[:, oc])
+    column_sums(ggain, gfw, GKC, pg)
+    column_sums(gain, fw, KC, pm)
+
     def arrived(j):
         d = (zl + 4 - j) % 4
         for e, h in enumerate((zh, oh)):
@@ -358,7 +395,7 @@
     send(r_mx[0], at.at[x, :, 0:3], at.at[x, :, 0:3], s, head_of(xp, zh))
     send(r_mx[1], at.at[x, :, 0:3], at.at[x, :, 0:3], s, head_of(xm, zh))
 
-    for r, buf in zip(r_w, (wt, gwt)):
+    for r, buf in ((r_w[1], gwt), (r_w[0], wt)):
         a, b = buf.at[ym, 0:2, c], buf.at[yp, 2:4, c]
         wait(r[0], buf.at[ym, :, c])
         send(r[2], a, a, seq_of(yp, zl, c), g)
@@ -372,12 +409,10 @@
     send(r_mx[2], at.at[xm, 0, 0:3], at.at[xm, 0, 0:3], s, head_of(xp, zh))
     wait(r_mx[1], at.at[xp, :, 0:3])
     send(r_mx[3], at.at[xp, 1, 0:3], at.at[xp, 1, 0:3], s, head_of(xm, zh))
-    for r, buf in zip(r_w, (wt, gwt)):
+    for r, buf in ((r_w[1], gwt), (r_w[0], wt)):
         wait(r[2], buf.at[y2, 0:2, c])
         wait(r[3], buf.at[y2, 2:4, c])
         send(r[4], buf.at[:, :, c], buf.at[:, :, c], seq_of(y, zl, oc), g)
-    wait(r_fc, fw.at[:, oc])
-    wait(r_gfc, gfw.at[:, oc])
     local[4].wait()
     local[5].wait()
 
@@ -397,17 +432,6 @@
             part = lax.dot_general(rows, block, NT, preferred_element_type=F32)
             total = part if total is None else total + part
         return total
-
-    def column_sums(gains, weights, width, keep):
-        n = width // 128
-        row = jnp.concatenate([gains[pl.ds(g * n + i, 1), :] for i in range(n)], axis=1)
-        rest = row - row.astype(BF16).astype(F32)
-        at_row = lax.broadcasted_iota(jnp.int32, (16, width), 0)
-        both = jnp.where(at_row == 0, row, jnp.where(at_row == 1, rest, 0.0)).astype(BF16)
-        sums = jnp.dot(both, weights[...].reshape(width, 64), preferred_element_type=F32)
-        sums = jnp.broadcast_to(jnp.sum(sums, axis=0, keepdims=True), (64, 64)).T
-        for i in range(8):
-            keep[i, 0:8, ROWS:] = sums[i * 8 : (i + 1) * 8]
 
     def spread(ref, width, gains, weights, keep, buf, roles):
         one = jnp.zeros((ROWS, 128), F32)
@@ -451,8 +475,7 @@
         return total * scale
 
     r_pg, r_pm, r_out = ([role() for _ in range(7)] for _ in range(3))
-    column_sums(ggain, gfw, GKC, pg)
-    column_sums(gain, fw, KC, pm)
+    sent_d = len(started)
     wait(r_w[1][4], gwt.at[:, :, oc])
     ghid[...] = gsb[...].astype(F32) + gout_part(x)
     ghid[...] += gout_part(xm)
@@ -461,20 +484,27 @@
     wait(r_gx[3], at.at[x2, 1, 3])
     ghid[...] += gout_part(x2)
     spread(ghid, GKC, ggain, gfw, pg, rg, r_pg)
-    wait(r_w[0][4], wt.at[:, :, oc])
-    hid[...] = sb[...].astype(F32) + out_part(x)
-    hid[...] += out_part(xm)
-    hid[...] += out_part(xp)
     gp[y, zl, c] = combine(GKC, rg, r_pg)
     near = [(d, e) for d in range(4) for e in range(2) if d or e]
     r_az, r_ay = [role() for _ in near], [role() for _ in range(3)]
     for r, (d, e) in zip(r_az, near):
         block = gp.at[y, zl, c]
         send(r, block, block, seq_of(y, (zl + d) % 4, oc if e else c), g)
+    wait(r_w[0][4], wt.at[:, :, oc])
+    hid[...] = sb[...].astype(F32) + out_part(x)
+    hid[...] += out_part(xm)
+    hid[...] += out_part(xp)
     wait(r_mx[2], at.at[x2, 0, 0:3])
     wait(r_mx[3], at.at[x2, 1, 0:3])
     hid[...] += out_part(x2)
     spread(hid, KC, gain, fw, pm, rm, r_pm)
+    flush(sent_d)
+
+    @pl.when(jnp.logical_not(same))
+    def _():
+        for r, (src, there, _) in zip(r_perm, moved):
+            copy(r, src, there, part_s, part_g).wait_send()
+
     for r, (d, e) in zip(r_az, near):
         wait(r, gp.at[y, (zl + 4 - d) % 4, oc if e else c])
     for d in (1, 2, 3):
@@ -505,18 +535,13 @@
     outb[g] = picked + strength * (main_pred - picked)
     for d in range(1, 8):
         send(r_out[d - 1], outb.at[g], outb.at[g], s, (g + d) % 8)
+    flush(len(started) - 7)
     for d in range(1, 8):
         wait(r_out[d - 1], outb.at[(g + 8 - d) % 8])
     for i in range(8):
         out[i * 8 : (i + 1) * 8, :] = outb[i]
 
-    for one in started:
-        one.wait_send()
-
-    @pl.when(jnp.logical_not(same))
-    def _():
-        for r, (src, there, _) in zip(r_perm, moved):
-            copy(r, src, there, part_s, part_g).wait_send()
+    flush(len(started))
 
 
 def per_device(

time: 133 us -> 127 us (0.955)
  Pallas kernels: 132 us -> 126 us
    pallas_call x1, Pallas kernels: 132 us -> 126 us  [per_device(): pl.pallas_call(body, out_shape=jax.ShapeDtypeStruct((64, ROWS), F32), in_...]
where the time goes in v5:
time: 127 us
  Pallas kernels  126 us (99%)
  local copies, waits for them, and re-layouts  1.47 us (1%)
    pallas_call x1, Pallas kernels, per_device(): pl.pallas_call(body, out_shape=jax.ShapeDtypeStruct((64, ROWS), F32), in_...  126 us

profile of v5, /device:TPU:1, one launch (start us, length us, event | category | flops | bytes accessed | tf_op | source)
XLA Modules:
  0.0 127.1 jit_solution(11081044333542379341)
XLA Ops:
  0.0 125.6 %shard_map.136 = f32[64,192]{1,0:T(8,128)} custom-call(bf16[192,640]{1,0:T(8,128)(2,1)} %stream.1, bf16[192,640]{1,0:T(8,128)(2,1)} %normed.1, bf16[3,5120,384]{2,1,0:T(8,128)(2,1)} %bitcast.10, bf16[160,384]{1,0:T(8,128)(2,1)} %bitcast.11, f32[40,128]{1,0:T(8,128)} %bitcast.15, bf16[64,160]{1,0:T(8,128)(2,1)} %bitcast.13, bf16[192,256]{1,0:T(8,128)(2,1)} %gstream.1, ...), custom_call_target="tpu_custom_call" | custom-call | flops 6000000000 | bytes 20000000 | tf_op jit(solution)/shard_map/pallas_call | solution.py:590
  125.6 1.5 %copy.16 = f32[192,64]{0,1:T(8,128)} copy(f32[192,64]{0,1:T(8,128)} %bitcast.9) | data formatting | bytes 98304
